TPU v7x, 512 devices: a whole 4x8x8 slice. The times are simulated.
512 devices in a mesh: gx: 64 (over y, z_lo, core), gy: 8 (over x, z_hi).
Axes of the slice: x: 4, y: 8, z: 8 (z_hi: 2, z_lo: 4; z = z_hi * 4 + z_lo), core: 2. Of those that a mesh axis runs over, the one named last changes fastest.
Arguments:
- populations: float32 [27, 128, 32, 1024], P(None, 'gx', None, 'gy'), may hold values from 0.002 to 0.45, as said below
- fluid_mask: int32 [128, 32, 1024], P('gx', None, 'gy'), may hold values 0 or 1
Outputs:
- evolved: float32 [27, 128, 32, 1024], P(None, 'gx', None, 'gy')
Inputs may be any that keep to these rules, and one draw needn't show every extreme that they name: `populations`: every population lies between 0.5 and 1.5 times its lattice weight, the weight being the product over the three components of 2/3 for 0 and 1/6 for -1 or 1.
All inputs are finite; a program needn't handle non-finite values. No bound on the sum of `fluid_mask` on one device may be relied on, other than what follows from the above.
Results may differ from a plain program's by a relative error of at most 0.0001.
Values sent between devices are 32-bit elements; how exact they have to be, the bound alone decides.
A program may use at most 64 MiB of HBM per device.

v0:
```python
import jax
import jax.numpy as jnp
from jax import lax
from jax.sharding import PartitionSpec as P

STEPS = 3


shear_rate = 1.6
body_force = 0.002


def with_halo(block, sides, width):
    for axis, dim in sides:
        count = lax.axis_size(axis)
        forward = [(i, i + 1) for i in range(count - 1)]
        forward.append((count - 1, 0))
        backward = [(target, source) for source, target in forward]
        low = lax.ppermute(
            lax.slice_in_dim(block, block.shape[dim] - width, None, axis=dim), axis, forward
        )
        high = lax.ppermute(lax.slice_in_dim(block, 0, width, axis=dim), axis, backward)
        block = jnp.concatenate([low, block, high], axis=dim)
    return block


def forward_triple(minus, rest, plus, speed):
    total = minus + rest + plus
    first = plus - minus
    second = plus + minus
    return (total, first - speed * total, second - 2.0 * speed * first + speed * speed * total)


def inverse_triple(zeroth, first, second, speed):
    raw_one = first + speed * zeroth
    raw_two = second + 2.0 * speed * first + speed * speed * zeroth
    return ((raw_two - raw_one) * 0.5, zeroth - raw_two, (raw_two + raw_one) * 0.5)


def collide(pops):
    density = jnp.sum(pops, axis=(0, 1, 2))
    speed_x = (jnp.sum(pops[2] - pops[0], axis=(0, 1)) + 0.5 * body_force) / density
    speed_y = jnp.sum(pops[:, 2] - pops[:, 0], axis=(0, 1)) / density
    speed_z = jnp.sum(pops[:, :, 2] - pops[:, :, 0], axis=(0, 1)) / density
    moments = jnp.stack(forward_triple(pops[0], pops[1], pops[2], speed_x), axis=0)
    moments = jnp.stack(
        forward_triple(moments[:, 0], moments[:, 1], moments[:, 2], speed_y), axis=1
    )
    moments = jnp.stack(
        forward_triple(moments[:, :, 0], moments[:, :, 1], moments[:, :, 2], speed_z), axis=2
    )
    keep = 1.0 - shear_rate
    trace = moments[2, 0, 0] + moments[0, 2, 0] + moments[0, 0, 2]
    s200 = keep * (moments[2, 0, 0] - trace / 3.0) + density / 3.0
    s020 = keep * (moments[0, 2, 0] - trace / 3.0) + density / 3.0
    s002 = keep * (moments[0, 0, 2] - trace / 3.0) + density / 3.0
    s110 = keep * moments[1, 1, 0]
    s101 = keep * moments[1, 0, 1]
    s011 = keep * moments[0, 1, 1]
    entries = {
        (0, 0, 0): density,
        (1, 0, 0): -moments[1, 0, 0],
        (0, 1, 0): -moments[0, 1, 0],
        (0, 0, 1): -moments[0, 0, 1],
        (2, 0, 0): s200,
        (0, 2, 0): s020,
        (0, 0, 2): s002,
        (1, 1, 0): s110,
        (1, 0, 1): s101,
        (0, 1, 1): s011,
        (2, 2, 0): (s200 * s020 + 2.0 * s110 * s110) / density,
        (2, 0, 2): (s200 * s002 + 2.0 * s101 * s101) / density,
        (0, 2, 2): (s020 * s002 + 2.0 * s011 * s011) / density,
        (2, 1, 1): (s200 * s011 + 2.0 * s110 * s101) / density,
        (1, 2, 1): (s020 * s101 + 2.0 * s110 * s011) / density,
        (1, 1, 2): (s002 * s110 + 2.0 * s101 * s011) / density,
        (2, 2, 2): (
            s200 * s020 * s002
            + 2.0 * s110 * s110 * s002
            + 2.0 * s101 * s101 * s020
            + 2.0 * s011 * s011 * s200
            + 8.0 * s110 * s101 * s011
        )
        / (density * density),
    }
    nothing = jnp.zeros_like(density)
    post = jnp.stack(
        [
            jnp.stack(
                [
                    jnp.stack(
                        [entries.get((along_x, along_y, along_z), nothing) for along_z in range(3)]
                    )
                    for along_y in range(3)
                ]
            )
            for along_x in range(3)
        ]
    )
    back = jnp.stack(inverse_triple(post[:, :, 0], post[:, :, 1], post[:, :, 2], speed_z), axis=2)
    back = jnp.stack(inverse_triple(back[:, 0], back[:, 1], back[:, 2], speed_y), axis=1)
    back = jnp.stack(inverse_triple(back[0], back[1], back[2], speed_x), axis=0)
    return back


def relax(pops, fluid):
    return jnp.where(fluid, collide(pops), pops[::-1, ::-1, ::-1])


def stream(padded, width_x, depth, width_y):
    pieces = []
    for along_x in range(3):
        for along_y in range(3):
            for along_z in range(3):
                piece = padded[
                    along_x,
                    along_y,
                    along_z,
                    2 - along_x : 2 - along_x + width_x,
                    :,
                    2 - along_y : 2 - along_y + width_y,
                ]
                pieces.append(jnp.roll(piece, along_z - 1, axis=1))
    return jnp.stack(pieces).reshape(3, 3, 3, width_x, depth, width_y)


def on_device(populations, fluid_mask):
    width_x, depth, width_y = fluid_mask.shape
    fluid = fluid_mask == 1
    pops = populations.reshape(3, 3, 3, width_x, depth, width_y)
    for step_index in range(STEPS):
        post = relax(pops, fluid)
        padded = with_halo(post.reshape(27, width_x, depth, width_y), (("gx", 1), ("gy", 3)), 1)
        padded = padded.reshape(3, 3, 3, width_x + 2, depth, width_y + 2)
        pops = stream(padded, width_x, depth, width_y)
    return pops.reshape(27, width_x, depth, width_y)


def solution(mesh):
    in_specs = (P(None, "gx", None, "gy"), P("gx", None, "gy"))
    out_specs = P(None, "gx", None, "gy")
    return jax.shard_map(
        on_device, mesh=mesh, in_specs=in_specs, out_specs=out_specs, check_vma=False
    )
```

profile of v0, /device:TPU:1, one launch (start us, length us, event | category | flops | bytes accessed | tf_op | source)
XLA Modules:
  0.0 157.2 jit_solution(1923104009362327176)
XLA Ops:
  7.3 5.4 %collective-permute-start = (f32[27,1,32,128]{3,2,1,0:T(8,128)S(1)}, f32[27,1,32,128]{3,2,1,0:T(8,128)S(1)}, u32[]{:S(2)}, u32[]{:S(2)}) collective-permute-start(f32[27,1,32,128]{3,2,1,0:T(8,128)S(1)} %get-tuple-element.190), channel_id=1, source_target_pairs={{0,8},{8,16},{16,24},{24,32},{32,40},{40,48},{48,56},{56,64},{64,7... | collective-permute-start | bytes 1327112 | tf_op jit(solution)/shard_map/ppermute | solution.py:19
  12.7 5.3 %collective-permute-start.1 = (f32[27,1,32,128]{3,2,1,0:T(8,128)S(1)}, f32[27,1,32,128]{3,2,1,0:T(8,128)S(1)}, u32[]{:S(2)}, u32[]{:S(2)}) collective-permute-start(f32[27,1,32,128]{3,2,1,0:T(8,128)S(1)} %get-tuple-element.191), channel_id=1, source_target_pairs={{8,0},{16,8},{24,16},{32,24},{40,32},{48,40},{56,48},{64,56},{72,6... | collective-permute-start | bytes 1327112 | tf_op jit(solution)/shard_map/ppermute | solution.py:22
  18.0 4.6 %collective-permute-done.1 = f32[27,1,32,128]{3,2,1,0:T(8,128)S(1)} collective-permute-done((f32[27,1,32,128]{3,2,1,0:T(8,128)S(1)}, f32[27,1,32,128]{3,2,1,0:T(8,128)S(1)}, u32[]{:S(2)}, u32[]{:S(2)}) %collective-permute-start.1) | collective-permute-done | bytes 442400 | tf_op jit(solution)/shard_map/ppermute | solution.py:22
  24.6 2.8 %copy.387 = f32[27,4,32,1]{2,1,3,0:T(4,128)} copy(f32[27,4,32,1]{3,2,1,0:T(8,128)} %get-tuple-element.162) | data formatting | bytes 27648
  27.4 14.2 %collective-permute-start.2 = (f32[27,4,32,1]{2,1,3,0:T(4,128)}, f32[27,4,32,1]{2,1,3,0:T(4,128)}, u32[]{:S(2)}, u32[]{:S(2)}) collective-permute-start(f32[27,4,32,1]{2,1,3,0:T(4,128)} %copy.387), channel_id=1, source_target_pairs={{0,1},{1,2},{2,3},{3,4},{4,5},{5,6},{6,7},{7,0},{8,9},{9,10},{10,1... | collective-permute-start | bytes 41480 | tf_op jit(solution)/shard_map/ppermute | solution.py:19
  42.9 4.1 %collective-permute-start.3 = (f32[27,4,32,1]{2,1,3,0:T(4,128)}, f32[27,4,32,1]{2,1,3,0:T(4,128)}, u32[]{:S(2)}, u32[]{:S(2)}) collective-permute-start(f32[27,4,32,1]{2,1,3,0:T(4,128)} %copy.388), channel_id=1, source_target_pairs={{1,0},{2,1},{3,2},{4,3},{5,4},{6,5},{7,6},{0,7},{9,8},{10,9},{11,1... | collective-permute-start | bytes 41480 | tf_op jit(solution)/shard_map/ppermute | solution.py:22
  48.5 4.1 %collective-permute-done.3 = f32[27,4,32,1]{2,1,3,0:T(4,128)} collective-permute-done((f32[27,4,32,1]{2,1,3,0:T(4,128)}, f32[27,4,32,1]{2,1,3,0:T(4,128)}, u32[]{:S(2)}, u32[]{:S(2)}) %collective-permute-start.3) | collective-permute-done | bytes 13856 | tf_op jit(solution)/shard_map/ppermute | solution.py:22
  52.6 2.7 %copy.338 = f32[27,4,32,1]{3,2,1,0:T(8,128)} copy(f32[27,4,32,1]{2,1,3,0:T(4,128)} %collective-permute-done.3) | data formatting | bytes 27648 | tf_op jit(solution)/shard_map/ppermute | solution.py:22
  55.3 2.9 %pad_maximum_fusion = f32[27,4,32,130]{3,2,1,0:T(8,128)S(1)} fusion(f32[27,4,32,1]{3,2,1,0:T(8,128)} %copy.338, f32[27,1,32,128]{3,2,1,0:T(8,128)S(1)} %collective-permute-done.1, f32[27,2,32,128]{3,2,1,0:T(8,128)S(1)} %bitcast.1235, f32[27,1,32,128]{3,2,1,0:T(8,128)S(1)} %collective-permute-done, f32[27,4,32,1]{3,2,1,0:T(8,128)S(1)} %copy.337), kind=kLoop, calls=%fused_computation | loop fusion | flops 1797120 | bytes 3594240 | tf_op jit(solution)/shard_map/concatenate | solution.py:23
  63.2 4.2 %collective-permute-start.4 = (f32[27,1,32,128]{3,2,1,0:T(8,128)S(1)}, f32[27,1,32,128]{3,2,1,0:T(8,128)S(1)}, u32[]{:S(2)}, u32[]{:S(2)}) collective-permute-start(f32[27,1,32,128]{3,2,1,0:T(8,128)S(1)} %get-tuple-element.186), channel_id=1, source_target_pairs={{0,8},{8,16},{16,24},{24,32},{32,40},{40,48},{48,56},{56,64},{64,7... | collective-permute-start | bytes 1327112 | tf_op jit(solution)/shard_map/ppermute | solution.py:19
  69.3 8.0 %collective-permute-done.4 = f32[27,1,32,128]{3,2,1,0:T(8,128)S(1)} collective-permute-done((f32[27,1,32,128]{3,2,1,0:T(8,128)S(1)}, f32[27,1,32,128]{3,2,1,0:T(8,128)S(1)}, u32[]{:S(2)}, u32[]{:S(2)}) %collective-permute-start.4) | collective-permute-done | bytes 442400 | tf_op jit(solution)/shard_map/ppermute | solution.py:19
  81.8 2.8 %copy.391 = f32[27,4,32,1]{2,1,3,0:T(4,128)} copy(f32[27,4,32,1]{3,2,1,0:T(8,128)} %get-tuple-element.160) | data formatting | bytes 27648
  84.6 3.0 %collective-permute-start.6 = (f32[27,4,32,1]{2,1,3,0:T(4,128)}, f32[27,4,32,1]{2,1,3,0:T(4,128)}, u32[]{:S(2)}, u32[]{:S(2)}) collective-permute-start(f32[27,4,32,1]{2,1,3,0:T(4,128)} %copy.391), channel_id=1, source_target_pairs={{0,1},{1,2},{2,3},{3,4},{4,5},{5,6},{6,7},{7,0},{8,9},{9,10},{10,1... | collective-permute-start | bytes 41480 | tf_op jit(solution)/shard_map/ppermute | solution.py:19
  88.9 8.4 %collective-permute-start.7 = (f32[27,4,32,1]{2,1,3,0:T(4,128)}, f32[27,4,32,1]{2,1,3,0:T(4,128)}, u32[]{:S(2)}, u32[]{:S(2)}) collective-permute-start(f32[27,4,32,1]{2,1,3,0:T(4,128)} %copy.392), channel_id=1, source_target_pairs={{1,0},{2,1},{3,2},{4,3},{5,4},{6,5},{7,6},{0,7},{9,8},{10,9},{11,1... | collective-permute-start | bytes 41480 | tf_op jit(solution)/shard_map/ppermute | solution.py:22
  98.9 2.7 %copy.362 = f32[27,4,32,1]{3,2,1,0:T(8,128)} copy(f32[27,4,32,1]{2,1,3,0:T(4,128)} %collective-permute-done.7) | data formatting | bytes 27648 | tf_op jit(solution)/shard_map/ppermute | solution.py:22
  101.6 2.9 %pad_maximum_fusion.1 = f32[27,4,32,130]{3,2,1,0:T(8,128)S(1)} fusion(f32[27,4,32,1]{3,2,1,0:T(8,128)} %copy.362, f32[27,1,32,128]{3,2,1,0:T(8,128)S(1)} %collective-permute-done.5, f32[27,2,32,128]{3,2,1,0:T(8,128)S(1)} %bitcast.1232, f32[27,1,32,128]{3,2,1,0:T(8,128)S(1)} %collective-permute-done.4, f32[27,4,32,1]{3,2,1,0:T(8,128)S(1)} %copy.361), kind=kLoop, calls=%fused_computation.1 | loop fusion | flops 1797120 | bytes 3594240 | tf_op jit(solution)/shard_map/concatenate | solution.py:23
  109.5 3.8 %collective-permute-start.8 = (f32[27,1,32,128]{3,2,1,0:T(8,128)S(1)}, f32[27,1,32,128]{3,2,1,0:T(8,128)S(1)}, u32[]{:S(2)}, u32[]{:S(2)}) collective-permute-start(f32[27,1,32,128]{3,2,1,0:T(8,128)S(1)} %get-tuple-element.182), channel_id=1, source_target_pairs={{0,8},{8,16},{16,24},{24,32},{32,40},{40,48},{48,56},{56,64},{64,7... | collective-permute-start | bytes 1327112 | tf_op jit(solution)/shard_map/ppermute | solution.py:19
  115.3 8.0 %collective-permute-done.8 = f32[27,1,32,128]{3,2,1,0:T(8,128)S(1)} collective-permute-done((f32[27,1,32,128]{3,2,1,0:T(8,128)S(1)}, f32[27,1,32,128]{3,2,1,0:T(8,128)S(1)}, u32[]{:S(2)}, u32[]{:S(2)}) %collective-permute-start.8) | collective-permute-done | bytes 442400 | tf_op jit(solution)/shard_map/ppermute | solution.py:19
  127.9 2.8 %copy.395 = f32[27,4,32,1]{2,1,3,0:T(4,128)} copy(f32[27,4,32,1]{3,2,1,0:T(8,128)} %get-tuple-element.158) | data formatting | bytes 27648
  130.7 7.6 %collective-permute-start.10 = (f32[27,4,32,1]{2,1,3,0:T(4,128)}, f32[27,4,32,1]{2,1,3,0:T(4,128)}, u32[]{:S(2)}, u32[]{:S(2)}) collective-permute-start(f32[27,4,32,1]{2,1,3,0:T(4,128)} %copy.395), channel_id=1, source_target_pairs={{0,1},{1,2},{2,3},{3,4},{4,5},{5,6},{6,7},{7,0},{8,9},{9,10},{10,1... | collective-permute-start | bytes 41480 | tf_op jit(solution)/shard_map/ppermute | solution.py:19
  139.7 4.4 %collective-permute-start.11 = (f32[27,4,32,1]{2,1,3,0:T(4,128)}, f32[27,4,32,1]{2,1,3,0:T(4,128)}, u32[]{:S(2)}, u32[]{:S(2)}) collective-permute-start(f32[27,4,32,1]{2,1,3,0:T(4,128)} %copy.396), channel_id=1, source_target_pairs={{1,0},{2,1},{3,2},{4,3},{5,4},{6,5},{7,6},{0,7},{9,8},{10,9},{11,1... | collective-permute-start | bytes 41480 | tf_op jit(solution)/shard_map/ppermute | solution.py:22
  145.6 3.2 %collective-permute-done.11 = f32[27,4,32,1]{2,1,3,0:T(4,128)} collective-permute-done((f32[27,4,32,1]{2,1,3,0:T(4,128)}, f32[27,4,32,1]{2,1,3,0:T(4,128)}, u32[]{:S(2)}, u32[]{:S(2)}) %collective-permute-start.11) | collective-permute-done | bytes 13856 | tf_op jit(solution)/shard_map/ppermute | solution.py:22
  148.8 2.7 %copy.386 = f32[27,4,32,1]{3,2,1,0:T(8,128)} copy(f32[27,4,32,1]{2,1,3,0:T(4,128)} %collective-permute-done.11) | data formatting | bytes 27648 | tf_op jit(solution)/shard_map/ppermute | solution.py:22
  151.5 2.9 %pad_maximum_fusion.2 = f32[27,4,32,130]{3,2,1,0:T(8,128)S(1)} fusion(f32[27,4,32,1]{3,2,1,0:T(8,128)} %copy.386, f32[27,1,32,128]{3,2,1,0:T(8,128)S(1)} %collective-permute-done.9, f32[27,2,32,128]{3,2,1,0:T(8,128)S(1)} %bitcast.1229, f32[27,1,32,128]{3,2,1,0:T(8,128)S(1)} %collective-permute-done.8, f32[27,4,32,1]{3,2,1,0:T(8,128)S(1)} %copy.385), kind=kLoop, calls=%fused_computation.2 | loop fusion | flops 1797120 | bytes 3594240 | tf_op jit(solution)/shard_map/concatenate | solution.py:23
  (364 shorter events, 41.2 us)
Async XLA Ops:
  0.0 4.3 %copy-start = (f32[27,2,32,128]{3,2,1,0:T(8,128)S(1)}, f32[27,2,32,128]{3,2,1,0:T(8,128)}, u32[]{:S(2)}) copy-start(f32[27,2,32,128]{3,2,1,0:T(8,128)} %param.2) | copy-start | bytes 2654212
  5.4 0.6 copy-start.1
  7.3 10.7 %collective-permute-start = (f32[27,1,32,128]{3,2,1,0:T(8,128)S(1)}, f32[27,1,32,128]{3,2,1,0:T(8,128)S(1)}, u32[]{:S(2)}, u32[]{:S(2)}) collective-permute-start(f32[27,1,32,128]{3,2,1,0:T(8,128)S(1)} %get-tuple-element.190), channel_id=1, source_target_pairs={{0,8},{8,16},{16,24},{24,32},{32,40},{40,48},{48,56},{56,64},{64,7... | collective-permute-start | bytes 1327112 | tf_op jit(solution)/shard_map/ppermute | solution.py:19
  12.7 9.9 %collective-permute-start.1 = (f32[27,1,32,128]{3,2,1,0:T(8,128)S(1)}, f32[27,1,32,128]{3,2,1,0:T(8,128)S(1)}, u32[]{:S(2)}, u32[]{:S(2)}) collective-permute-start(f32[27,1,32,128]{3,2,1,0:T(8,128)S(1)} %get-tuple-element.191), channel_id=1, source_target_pairs={{8,0},{16,8},{24,16},{32,24},{40,32},{48,40},{56,48},{64,56},{72,6... | collective-permute-start | bytes 1327112 | tf_op jit(solution)/shard_map/ppermute | solution.py:22
  27.4 19.6 %collective-permute-start.2 = (f32[27,4,32,1]{2,1,3,0:T(4,128)}, f32[27,4,32,1]{2,1,3,0:T(4,128)}, u32[]{:S(2)}, u32[]{:S(2)}) collective-permute-start(f32[27,4,32,1]{2,1,3,0:T(4,128)} %copy.387), channel_id=1, source_target_pairs={{0,1},{1,2},{2,3},{3,4},{4,5},{5,6},{6,7},{7,0},{8,9},{9,10},{10,1... | collective-permute-start | bytes 41480 | tf_op jit(solution)/shard_map/ppermute | solution.py:19
  42.9 9.7 %collective-permute-start.3 = (f32[27,4,32,1]{2,1,3,0:T(4,128)}, f32[27,4,32,1]{2,1,3,0:T(4,128)}, u32[]{:S(2)}, u32[]{:S(2)}) collective-permute-start(f32[27,4,32,1]{2,1,3,0:T(4,128)} %copy.388), channel_id=1, source_target_pairs={{1,0},{2,1},{3,2},{4,3},{5,4},{6,5},{7,6},{0,7},{9,8},{10,9},{11,1... | collective-permute-start | bytes 41480 | tf_op jit(solution)/shard_map/ppermute | solution.py:22
  61.1 0.8 copy-start.2
  63.2 14.1 %collective-permute-start.4 = (f32[27,1,32,128]{3,2,1,0:T(8,128)S(1)}, f32[27,1,32,128]{3,2,1,0:T(8,128)S(1)}, u32[]{:S(2)}, u32[]{:S(2)}) collective-permute-start(f32[27,1,32,128]{3,2,1,0:T(8,128)S(1)} %get-tuple-element.186), channel_id=1, source_target_pairs={{0,8},{8,16},{16,24},{24,32},{32,40},{40,48},{48,56},{56,64},{64,7... | collective-permute-start | bytes 1327112 | tf_op jit(solution)/shard_map/ppermute | solution.py:19
  67.4 12.3 %collective-permute-start.5 = (f32[27,1,32,128]{3,2,1,0:T(8,128)S(1)}, f32[27,1,32,128]{3,2,1,0:T(8,128)S(1)}, u32[]{:S(2)}, u32[]{:S(2)}) collective-permute-start(f32[27,1,32,128]{3,2,1,0:T(8,128)S(1)} %get-tuple-element.187), channel_id=1, source_target_pairs={{8,0},{16,8},{24,16},{32,24},{40,32},{48,40},{56,48},{64,56},{72,6... | collective-permute-start | bytes 1327112 | tf_op jit(solution)/shard_map/ppermute | solution.py:22
  84.6 12.8 %collective-permute-start.6 = (f32[27,4,32,1]{2,1,3,0:T(4,128)}, f32[27,4,32,1]{2,1,3,0:T(4,128)}, u32[]{:S(2)}, u32[]{:S(2)}) collective-permute-start(f32[27,4,32,1]{2,1,3,0:T(4,128)} %copy.391), channel_id=1, source_target_pairs={{0,1},{1,2},{2,3},{3,4},{4,5},{5,6},{6,7},{7,0},{8,9},{9,10},{10,1... | collective-permute-start | bytes 41480 | tf_op jit(solution)/shard_map/ppermute | solution.py:19
  88.9 10.0 %collective-permute-start.7 = (f32[27,4,32,1]{2,1,3,0:T(4,128)}, f32[27,4,32,1]{2,1,3,0:T(4,128)}, u32[]{:S(2)}, u32[]{:S(2)}) collective-permute-start(f32[27,4,32,1]{2,1,3,0:T(4,128)} %copy.392), channel_id=1, source_target_pairs={{1,0},{2,1},{3,2},{4,3},{5,4},{6,5},{7,6},{0,7},{9,8},{10,9},{11,1... | collective-permute-start | bytes 41480 | tf_op jit(solution)/shard_map/ppermute | solution.py:22
  107.4 0.8 copy-start.3
  109.5 13.8 %collective-permute-start.8 = (f32[27,1,32,128]{3,2,1,0:T(8,128)S(1)}, f32[27,1,32,128]{3,2,1,0:T(8,128)S(1)}, u32[]{:S(2)}, u32[]{:S(2)}) collective-permute-start(f32[27,1,32,128]{3,2,1,0:T(8,128)S(1)} %get-tuple-element.182), channel_id=1, source_target_pairs={{0,8},{8,16},{16,24},{24,32},{32,40},{40,48},{48,56},{56,64},{64,7... | collective-permute-start | bytes 1327112 | tf_op jit(solution)/shard_map/ppermute | solution.py:19
  113.3 12.6 %collective-permute-start.9 = (f32[27,1,32,128]{3,2,1,0:T(8,128)S(1)}, f32[27,1,32,128]{3,2,1,0:T(8,128)S(1)}, u32[]{:S(2)}, u32[]{:S(2)}) collective-permute-start(f32[27,1,32,128]{3,2,1,0:T(8,128)S(1)} %get-tuple-element.183), channel_id=1, source_target_pairs={{8,0},{16,8},{24,16},{32,24},{40,32},{48,40},{56,48},{64,56},{72,6... | collective-permute-start | bytes 1327112 | tf_op jit(solution)/shard_map/ppermute | solution.py:22
  130.7 13.4 %collective-permute-start.10 = (f32[27,4,32,1]{2,1,3,0:T(4,128)}, f32[27,4,32,1]{2,1,3,0:T(4,128)}, u32[]{:S(2)}, u32[]{:S(2)}) collective-permute-start(f32[27,4,32,1]{2,1,3,0:T(4,128)} %copy.395), channel_id=1, source_target_pairs={{0,1},{1,2},{2,3},{3,4},{4,5},{5,6},{6,7},{7,0},{8,9},{9,10},{10,1... | collective-permute-start | bytes 41480 | tf_op jit(solution)/shard_map/ppermute | solution.py:19
  139.7 9.1 %collective-permute-start.11 = (f32[27,4,32,1]{2,1,3,0:T(4,128)}, f32[27,4,32,1]{2,1,3,0:T(4,128)}, u32[]{:S(2)}, u32[]{:S(2)}) collective-permute-start(f32[27,4,32,1]{2,1,3,0:T(4,128)} %copy.396), channel_id=1, source_target_pairs={{1,0},{2,1},{3,2},{4,3},{5,4},{6,5},{7,6},{0,7},{9,8},{10,9},{11,1... | collective-permute-start | bytes 41480 | tf_op jit(solution)/shard_map/ppermute | solution.py:22
  155.7 0.9 copy-start.4
where the time goes:
time: 160 us; the launch traced here: 157 us
  starting transfers between devices  64.3 us (40%)
  local copies, waits for them, and re-layouts  35.5 us (22%)
  waiting for transfers between devices  32.9 us (21%)
  other arithmetic  22.1 us (14%)
  between operations  2.45 us (2%)
    ppermute x6, starting transfers between devices, with_halo(): lax.ppermute(lax.slice_in_dim(block, block.shape[dim] - width, None, axis...  38.2 us
    ppermute x6, starting transfers between devices, with_halo(): lax.ppermute(lax.slice_in_dim(block, 0, width, axis=dim), axis, backward)  26.1 us
    ppermute x6, waiting for transfers between devices, with_halo(): lax.ppermute(lax.slice_in_dim(block, 0, width, axis=dim), axis, backward)  16.8 us
    ppermute x6, waiting for transfers between devices, with_halo(): lax.ppermute(lax.slice_in_dim(block, block.shape[dim] - width, None, axis...  16.1 us
    unnamed x51, local copies, waits for them, and re-layouts  15.9 us
    concatenate x6, other arithmetic, with_halo(): block = jnp.concatenate([low, block, high], axis=dim)  9.25 us
    ppermute x3, local copies, waits for them, and re-layouts, with_halo(): lax.ppermute(lax.slice_in_dim(block, 0, width, axis=dim), axis, backward)  8.19 us
    slice x6, local copies, waits for them, and re-layouts, with_halo(): lax.slice_in_dim(block, block.shape[dim] - width, None, axis=dim)  5.68 us
  transfers between devices with their start and end apart: 12, of which 7 were waited for; matrix products, arithmetic and copies ran while one was open for 5% of the time, Pallas kernels for 0%

commit v1 on v0

v1 whole, which is shorter than its diff:
```python
import jax
import jax.numpy as jnp
from jax import lax
from jax.experimental import pallas as pl
from jax.experimental.pallas import tpu as pltpu
from jax.sharding import PartitionSpec as P

STEPS = 3
MESH = pl.DeviceIdType.MESH

shear_rate = 1.6
body_force = 0.002
keep = 1.0 - shear_rate
third = 1.0 / 3.0

PAD = 8
NINE = 9


def inverse_triple(zeroth, first, second, speed):
    if zeroth is None:
        raw_one = first
        raw_two = 2.0 * speed * first
        rest = -raw_two
    else:
        if first is None:
            raw_one = speed * zeroth
            raw_two = second + speed * raw_one
        else:
            raw_one = first + speed * zeroth
            raw_two = speed * (first + raw_one)
            if second is not None:
                raw_two = second + raw_two
        rest = zeroth - raw_two
    plus = 0.5 * (raw_two + raw_one)
    return plus - raw_one, rest, plus


def collide(f):
    g = [[[f[9 * a + 3 * b + c] for c in range(3)] for b in range(3)] for a in range(3)]
    even = [[g[2][b][c] + g[0][b][c] for c in range(3)] for b in range(3)]
    diff = [[g[2][b][c] - g[0][b][c] for c in range(3)] for b in range(3)]
    total = [[even[b][c] + g[1][b][c] for c in range(3)] for b in range(3)]
    t_even = [total[2][c] + total[0][c] for c in range(3)]
    t_diff = [total[2][c] - total[0][c] for c in range(3)]
    t_total = [t_even[c] + total[1][c] for c in range(3)]
    d_total = [diff[2][c] + diff[0][c] + diff[1][c] for c in range(3)]
    d_diff = [diff[2][c] - diff[0][c] for c in range(3)]
    e_total = [even[2][c] + even[0][c] + even[1][c] for c in range(3)]
    m002 = t_total[2] + t_total[0]
    jz = t_total[2] - t_total[0]
    rho = m002 + t_total[1]
    jy = t_diff[0] + t_diff[1] + t_diff[2]
    m011 = t_diff[2] - t_diff[0]
    m020 = t_even[0] + t_even[1] + t_even[2]
    jx = d_total[0] + d_total[1] + d_total[2]
    m101 = d_total[2] - d_total[0]
    m110 = d_diff[0] + d_diff[1] + d_diff[2]
    m200 = e_total[0] + e_total[1] + e_total[2]
    r = 1.0 / rho
    ux = (jx + 0.5 * body_force) * r
    uy = jy * r
    uz = jz * r
    s100 = ux * rho - jx
    s010 = uy * rho - jy
    s001 = uz * rho - jz
    k200 = m200 - ux * (jx - s100)
    k020 = m020 - uy * (jy - s010)
    k002 = m002 - uz * (jz - s001)
    k110 = m110 - ux * jy + uy * s100
    k101 = m101 - ux * jz + uz * s100
    k011 = m011 - uy * jz + uz * s010
    base = third * rho - (keep * third) * (k200 + k020 + k002)
    s200 = keep * k200 + base
    s020 = keep * k020 + base
    s002 = keep * k002 + base
    s110 = keep * k110
    s101 = keep * k101
    s011 = keep * k011
    d110 = 2.0 * s110
    d101 = 2.0 * s101
    d011 = 2.0 * s011
    q110 = d110 * s110
    q101 = d101 * s101
    q011 = d011 * s011
    p220 = s200 * s020 + q110
    s220 = p220 * r
    s202 = (s200 * s002 + q101) * r
    s022 = (s020 * s002 + q011) * r
    s211 = (s200 * s011 + d110 * s101) * r
    s121 = (s020 * s101 + d110 * s011) * r
    s112 = (s002 * s110 + d101 * s011) * r
    s222 = (p220 * s002 + q101 * s020 + q011 * s200 + 2.0 * d110 * s101 * d011) * (r * r)
    along_z = [[None] * 3 for _ in range(3)]
    along_z[0][0] = inverse_triple(rho, s001, s002, uz)
    along_z[1][0] = inverse_triple(s100, s101, None, uz)
    along_z[0][1] = inverse_triple(s010, s011, None, uz)
    along_z[2][0] = inverse_triple(s200, None, s202, uz)
    along_z[0][2] = inverse_triple(s020, None, s022, uz)
    along_z[1][1] = inverse_triple(s110, None, s112, uz)
    along_z[2][1] = inverse_triple(None, s211, None, uz)
    along_z[1][2] = inverse_triple(None, s121, None, uz)
    along_z[2][2] = inverse_triple(s220, None, s222, uz)
    out = [None] * 27
    for c in range(3):
        along_y = [
            inverse_triple(along_z[a][0][c], along_z[a][1][c], along_z[a][2][c], uy)
            for a in range(3)
        ]
        for b in range(3):
            triple = inverse_triple(along_y[0][b], along_y[1][b], along_y[2][b], ux)
            for a in range(3):
                out[9 * a + 3 * b + c] = triple[a]
    return out


def kernel(count_x, count_y, f_hbm, m_hbm, o_hbm, f, mask, post, edge, near, halo, out,
           in_sem, out_sem, x_send, x_recv, y_send, y_recv):
    gx, gy = lax.axis_index("gx"), lax.axis_index("gy")
    core = lax.rem(gx, 2)
    depth = mask.shape[1]
    tiles = depth // 8

    def device(dx, dy):
        return (lax.rem(gx + dx + count_x, count_x), lax.rem(gy + dy + count_y, count_y))

    outer, inner = core, 1 - core
    loads = []
    for k, p in enumerate((outer, inner)):
        loads.append(
            (
                pltpu.make_async_copy(f_hbm.at[:, p], f.at[:, p], in_sem.at[2 * k]),
                pltpu.make_async_copy(m_hbm.at[p], mask.at[p], in_sem.at[2 * k + 1]),
            )
        )
        for copy in loads[-1]:
            copy.start()

    barrier = pltpu.get_barrier_semaphore()
    for dx in (-1, 0, 1):
        for dy in (-1, 0, 1):
            if dx or dy:
                pl.semaphore_signal(barrier, inc=1, device_id=device(dx, dy), device_id_type=MESH)

    lane = lax.broadcasted_iota(jnp.int32, (8, 128), 1)

    def x_copy(s, up):
        lo = 18 if up else 0
        here, there = (2, 0) if up else (1, 3)
        return pltpu.make_async_remote_copy(
            src_ref=post.at[s, pl.ds(lo, NINE), here, pl.ds(PAD, depth)],
            dst_ref=post.at[s, pl.ds(lo, NINE), there, pl.ds(PAD, depth)],
            send_sem=x_send.at[s, up],
            recv_sem=x_recv.at[s, up],
            device_id=device(1 if up else -1, 0),
            device_id_type=MESH,
        )

    def y_copy(s, up, dx):
        return pltpu.make_async_remote_copy(
            src_ref=edge.at[s, up],
            dst_ref=near.at[s, up, 1 - dx],
            send_sem=y_send.at[s, up, dx + 1],
            recv_sem=y_recv.at[s, up, 1 - dx],
            device_id=device(dx, 1 if up else -1),
            device_id_type=MESH,
        )

    def streamed(s, p, row):
        sides = [None, None]
        for up in (0, 1):
            sides[up] = [
                pltpu.roll(
                    halo[up, pl.ds(PAD + row - cz, 8), :], lax.rem(128 - NINE * p, 128), axis=1
                )
                for cz in (-1, 0, 1)
            ]
        pops = []
        for index in range(27):
            cx, cy, cz = index // 9 - 1, index // 3 % 3 - 1, index % 3 - 1
            value = post[s, index, p + 1 - cx, pl.ds(PAD + row - cz, 8), :]
            if cy:
                up = 1 if cy > 0 else 0
                place = (1 - cx) * NINE + 3 * (cx + 1) + cz + 1
                end = 0 if up else 127
                value = jnp.where(
                    lane == end,
                    pltpu.roll(sides[up][cz + 1], (end - place) % 128, axis=1),
                    pltpu.roll(value, 1 if up else 127, axis=1),
                )
            pops.append(value)
        return pops

    def relax(s, p, j):
        row = pl.multiple_of(8 * j, 8)
        if s == 0:
            pops = [f[index, p, pl.ds(row, 8), :] for index in range(27)]
        else:
            pops = streamed(s - 1, p, row)
        fluid = mask[p, pl.ds(row, 8), :] == 1
        after = collide(pops)
        after = [jnp.where(fluid, after[index], pops[26 - index]) for index in range(27)]
        again = jnp.where(j == 0, PAD + depth, jnp.where(j == tiles - 1, 0, PAD + row))
        again = pl.multiple_of(again, 8)
        for index in range(27):
            post[s, index, p + 1, pl.ds(PAD + row, 8), :] = after[index]
            post[s, index, p + 1, pl.ds(again, 8), :] = after[index]
        for up in (0, 1):
            packed = jnp.zeros((8, 128), jnp.float32)
            for k in range(NINE):
                index = 9 * (k // 3) + 6 * up + k % 3
                start = 127 if up else 0
                packed = jnp.where(
                    lane == k, pltpu.roll(after[index], (k - start) % 128, axis=1), packed
                )
            edge[s, up] = edge[s, up] + pltpu.roll(packed, NINE * (2 * j + p), axis=1)

    def sweep(s, p):
        def body(j, carry):
            relax(s, p, j)
            return carry

        lax.fori_loop(0, tiles, body, 0)

    def send(s, up):
        x_copy(s, up).start()

    def receive(s):
        for up in (0, 1):
            for dx in (-1, 0, 1):
                y_copy(s, up, dx).wait_recv()
        for up in (0, 1):
            for j in range(tiles):
                base = 2 * NINE * j
                low = pltpu.roll(near[s, up, 0], (-base - NINE) % 128, axis=1)
                mid = pltpu.roll(near[s, up, 1], (NINE - base) % 128, axis=1)
                high = pltpu.roll(near[s, up, 2], (3 * NINE - base) % 128, axis=1)
                rows = jnp.where(lane < NINE, low, jnp.where(lane < 3 * NINE, mid, high))
                halo[up, PAD + 8 * j : PAD + 8 * j + 8, :] = rows
                if j == 0:
                    halo[up, PAD + depth : PAD + depth + 8, :] = rows
                if j == tiles - 1:
                    halo[up, 0:8, :] = rows
        for up in (0, 1):
            x_copy(s, up).wait_recv()
            there, lo = (0, 18) if up else (3, 0)
            for index in range(lo, lo + NINE):
                post[s, index, there, 0:8, :] = post[s, index, there, depth : depth + 8, :]
                post[s, index, there, PAD + depth : PAD + depth + 8, :] = post[
                    s, index, there, PAD : PAD + 8, :
                ]

    edge[...] = jnp.zeros_like(edge)
    for s in range(STEPS):
        if s:
            receive(s - 1)
        else:
            for copy in loads[0]:
                copy.wait()
        sweep(s, outer)
        if s == 0:
            pl.semaphore_wait(barrier, 8)

        @pl.when(core == 0)
        def _():
            send(s, 0)

        @pl.when(core == 1)
        def _():
            send(s, 1)

        if s == 0:
            for copy in loads[1]:
                copy.wait()
        sweep(s, inner)
        for up in (0, 1):
            for dx in (-1, 0, 1):
                y_copy(s, up, dx).start()

        @pl.when(core == 0)
        def _():
            send(s, 1)

        @pl.when(core == 1)
        def _():
            send(s, 0)

    receive(STEPS - 1)

    def finish(j, carry):
        row = pl.multiple_of(8 * j, 8)
        for p in (0, 1):
            for index, value in enumerate(streamed(STEPS - 1, p, row)):
                out[index, p, pl.ds(row, 8), :] = value
        return carry

    stores = []
    for j in range(tiles):
        finish(j, 0)
        copy = pltpu.make_async_copy(
            out.at[:, :, pl.ds(8 * j, 8)], o_hbm.at[:, :, pl.ds(8 * j, 8)], out_sem.at[j]
        )
        copy.start()
        stores.append(copy)
    for s in range(STEPS):
        for up in (0, 1):
            x_copy(s, up).wait_send()
            for dx in (-1, 0, 1):
                y_copy(s, up, dx).wait_send()
    for copy in stores:
        copy.wait()


def solution(mesh):
    count_x, count_y = mesh.shape["gx"], mesh.shape["gy"]

    def on_device(populations, fluid_mask):
        width_x, depth, width_y = fluid_mask.shape
        tall = depth + 2 * PAD

        def body(*refs):
            kernel(count_x, count_y, *refs)

        return pl.pallas_call(
            body,
            out_shape=jax.ShapeDtypeStruct(populations.shape, jnp.float32),
            in_specs=[pl.BlockSpec(memory_space=pl.ANY)] * 2,
            out_specs=pl.BlockSpec(memory_space=pl.ANY),
            scratch_shapes=[
                pltpu.VMEM(populations.shape, jnp.float32),
                pltpu.VMEM(fluid_mask.shape, jnp.int32),
                pltpu.VMEM((STEPS, 27, width_x + 2, tall, width_y), jnp.float32),
                pltpu.VMEM((STEPS, 2, 8, 128), jnp.float32),
                pltpu.VMEM((STEPS, 2, 3, 8, 128), jnp.float32),
                pltpu.VMEM((2, tall, 128), jnp.float32),
                pltpu.VMEM(populations.shape, jnp.float32),
                pltpu.SemaphoreType.DMA((4,)),
                pltpu.SemaphoreType.DMA((depth // 8,)),
                pltpu.SemaphoreType.DMA((STEPS, 2)),
                pltpu.SemaphoreType.DMA((STEPS, 2)),
                pltpu.SemaphoreType.DMA((STEPS, 2, 3)),
                pltpu.SemaphoreType.DMA((STEPS, 2, 3)),
            ],
            compiler_params=pltpu.CompilerParams(
                collective_id=0, has_side_effects=True, vmem_limit_bytes=40 * 2**20
            ),
            cost_estimate=pl.CostEstimate(
                flops=500 * STEPS * fluid_mask.size,
                bytes_accessed=8 * populations.size,
                transcendentals=0,
            ),
            name="lattice_steps",
        )(populations, fluid_mask)

    in_specs = (P(None, "gx", None, "gy"), P("gx", None, "gy"))
    out_specs = P(None, "gx", None, "gy")
    return jax.shard_map(
        on_device, mesh=mesh, in_specs=in_specs, out_specs=out_specs, check_vma=False
    )
```

time: 160 us -> 45.9 us (0.29); the launches traced: 157 us -> 45.7 us
  starting transfers between devices: 64.3 us -> 0 us
  Pallas kernels: 0 us -> 42.9 us
  waiting for transfers between devices: 32.9 us -> 0 us
  local copies, waits for them, and re-layouts: 35.5 us -> 2.84 us
  other arithmetic: 22.1 us -> 0 us
  between operations: 2.45 us -> 0.01 us
    ppermute x12 -> x0, starting transfers between devices: 64.3 us -> none  [the longest x6 38.2 us: with_halo(): lax.ppermute(lax.slice_in_dim(block, block.shape[dim] - width, None, axis...]
    pallas_call x0 -> x1, Pallas kernels: none -> 42.9 us  [on_device(): pl.pallas_call(body, out_shape=jax.ShapeDtypeStruct(populations.shape, jn...]
    ppermute x12 -> x0, waiting for transfers between devices: 32.9 us -> none  [the longest x6 16.8 us: with_halo(): lax.ppermute(lax.slice_in_dim(block, 0, width, axis=dim), axis, backward)]
    unnamed x51 -> x5, local copies, waits for them, and re-layouts: 15.9 us -> 2.84 us
    ppermute x6 -> x0, local copies, waits for them, and re-layouts: 12.7 us -> none  [the longest x3 8.19 us: with_halo(): lax.ppermute(lax.slice_in_dim(block, 0, width, axis=dim), axis, backward)]
    concatenate x6 -> x0, other arithmetic: 9.25 us -> none  [with_halo(): block = jnp.concatenate([low, block, high], axis=dim)]
    slice x37 -> x0, local copies, waits for them, and re-layouts: 5.82 us -> none  [the longest x6 5.68 us: with_halo(): lax.slice_in_dim(block, block.shape[dim] - width, None, axis=dim)]
    reduce_sum x9 -> x0, other arithmetic: 2.58 us -> none  [the longest x3 1.26 us: collide(): speed_y = jnp.sum(pops[:, 2] - pops[:, 0], axis=(0, 1)) / density]
  transfers between devices with their start and end apart: 12 -> 0, of which waited for: 7 -> 0; matrix products, arithmetic and copies ran while one was open for 5% -> 0% of each run, Pallas kernels for 0% -> 0%
where the time goes in v1:
time: 45.9 us; the launch traced here: 45.7 us
  Pallas kernels  42.9 us (93%)
  local copies, waits for them, and re-layouts  2.84 us (6%)
    pallas_call x1, Pallas kernels, on_device(): pl.pallas_call(body, out_shape=jax.ShapeDtypeStruct(populations.shape, jn...  42.9 us
    unnamed x5, local copies, waits for them, and re-layouts  2.84 us

profile of v1, /device:TPU:1, one launch (start us, length us, event | category | flops | bytes accessed | tf_op | source)
XLA Modules:
  0.0 45.7 jit_solution(6926399573728361610)
XLA Ops:
  0.0 0.0 copy-start
  0.0 1.2 %copy-done = f32[27,2,32,128]{3,2,1,0:T(8,128)S(1)} copy-done((f32[27,2,32,128]{3,2,1,0:T(8,128)S(1)}, f32[27,2,32,128]{3,2,1,0:T(8,128)}, u32[]{:S(2)}) %copy-start) | copy-done | bytes 884760
  1.2 0.0 copy-start.1
  1.2 0.8 %copy-done.1 = s32[2,32,128]{2,1,0:T(8,128)S(1)} copy-done((s32[2,32,128]{2,1,0:T(8,128)S(1)}, s32[2,32,128]{2,1,0:T(8,128)}, u32[]{:S(2)}) %copy-start.1) | copy-done | bytes 32792
  1.9 42.9 %lattice_steps.1 = f32[27,2,32,128]{3,2,1,0:T(8,128)S(1)} custom-call(f32[27,2,32,128]{3,2,1,0:T(8,128)S(1)} %copy-done, s32[2,32,128]{2,1,0:T(8,128)S(1)} %copy-done.1), custom_call_target="tpu_custom_call" | custom-call | flops 12288000 | bytes 1769472 | tf_op jit(solution)/shard_map/lattice_steps/pallas_call | solution.py:324
  44.8 0.9 %copy.4 = f32[27,2,32,128]{3,2,1,0:T(8,128)} copy(f32[27,2,32,128]{3,2,1,0:T(8,128)S(1)} %lattice_steps.1) | data formatting | bytes 1769472
Async XLA Ops:
  0.0 1.2 %copy-start = (f32[27,2,32,128]{3,2,1,0:T(8,128)S(1)}, f32[27,2,32,128]{3,2,1,0:T(8,128)}, u32[]{:S(2)}) copy-start(f32[27,2,32,128]{3,2,1,0:T(8,128)} %refs_0_.1) | copy-start | bytes 2654212
  1.2 0.8 %copy-start.1 = (s32[2,32,128]{2,1,0:T(8,128)S(1)}, s32[2,32,128]{2,1,0:T(8,128)}, u32[]{:S(2)}) copy-start(s32[2,32,128]{2,1,0:T(8,128)} %refs_1_.1) | copy-start | bytes 98308

commit v2 on v1

v2 whole, which is shorter than its diff:
```python
import jax
import jax.numpy as jnp
from jax import lax
from jax.experimental import pallas as pl
from jax.experimental.pallas import tpu as pltpu
from jax.sharding import PartitionSpec as P

STEPS = 3
MESH = pl.DeviceIdType.MESH

shear_rate = 1.6
body_force = 0.002
keep = 1.0 - shear_rate
third = 1.0 / 3.0

PAD = 8
NINE = 9
NEIGHBOURS = [(dx, dy) for dx in (-1, 0, 1) for dy in (-1, 0, 1) if dx or dy]

OWN = {1: [(3, (4, 5))], 0: [(-1, (2,)), (2, (4,))], -1: [(-2, (1, 2))]}
SENT = {
    1: {1: (0, (0, 1, 2), 0, (0, 1, 2)), 0: (2, (3, 4), -3, (0, 1)), -1: (3, (5,), -5, (0,))},
    0: {-1: (-3, (0, 1, 2), 4, (4, 5, 6)), 0: (0, (3, 4), 2, (5, 6)), 1: (2, (5,), 1, (6,))},
}
MASK = 27


def inverse_triple(zeroth, first, second, speed):
    if zeroth is None:
        raw_one = first
        raw_two = 2.0 * speed * first
        rest = -raw_two
    else:
        if first is None:
            raw_one = speed * zeroth
            raw_two = second + speed * raw_one
        else:
            raw_one = first + speed * zeroth
            raw_two = speed * (first + raw_one)
            if second is not None:
                raw_two = second + raw_two
        rest = zeroth - raw_two
    plus = 0.5 * (raw_two + raw_one)
    return plus - raw_one, rest, plus


def collide(f):
    g = [[[f[9 * a + 3 * b + c] for c in range(3)] for b in range(3)] for a in range(3)]
    even = [[g[2][b][c] + g[0][b][c] for c in range(3)] for b in range(3)]
    diff = [[g[2][b][c] - g[0][b][c] for c in range(3)] for b in range(3)]
    total = [[even[b][c] + g[1][b][c] for c in range(3)] for b in range(3)]
    t_even = [total[2][c] + total[0][c] for c in range(3)]
    t_diff = [total[2][c] - total[0][c] for c in range(3)]
    t_total = [t_even[c] + total[1][c] for c in range(3)]
    d_total = [diff[2][c] + diff[0][c] + diff[1][c] for c in range(3)]
    d_diff = [diff[2][c] - diff[0][c] for c in range(3)]
    e_total = [even[2][c] + even[0][c] + even[1][c] for c in range(3)]
    m002 = t_total[2] + t_total[0]
    jz = t_total[2] - t_total[0]
    rho = m002 + t_total[1]
    jy = t_diff[0] + t_diff[1] + t_diff[2]
    m011 = t_diff[2] - t_diff[0]
    m020 = t_even[0] + t_even[1] + t_even[2]
    jx = d_total[0] + d_total[1] + d_total[2]
    m101 = d_total[2] - d_total[0]
    m110 = d_diff[0] + d_diff[1] + d_diff[2]
    m200 = e_total[0] + e_total[1] + e_total[2]
    r = 1.0 / rho
    ux = (jx + 0.5 * body_force) * r
    uy = jy * r
    uz = jz * r
    s100 = ux * rho - jx
    s010 = uy * rho - jy
    s001 = uz * rho - jz
    k200 = m200 - ux * (jx - s100)
    k020 = m020 - uy * (jy - s010)
    k002 = m002 - uz * (jz - s001)
    k110 = m110 - ux * jy + uy * s100
    k101 = m101 - ux * jz + uz * s100
    k011 = m011 - uy * jz + uz * s010
    base = third * rho - (keep * third) * (k200 + k020 + k002)
    s200 = keep * k200 + base
    s020 = keep * k020 + base
    s002 = keep * k002 + base
    s110 = keep * k110
    s101 = keep * k101
    s011 = keep * k011
    d110 = 2.0 * s110
    d101 = 2.0 * s101
    d011 = 2.0 * s011
    q110 = d110 * s110
    q101 = d101 * s101
    q011 = d011 * s011
    p220 = s200 * s020 + q110
    s220 = p220 * r
    s202 = (s200 * s002 + q101) * r
    s022 = (s020 * s002 + q011) * r
    s211 = (s200 * s011 + d110 * s101) * r
    s121 = (s020 * s101 + d110 * s011) * r
    s112 = (s002 * s110 + d101 * s011) * r
    s222 = (p220 * s002 + q101 * s020 + q011 * s200 + 2.0 * d110 * s101 * d011) * (r * r)
    along_z = [[None] * 3 for _ in range(3)]
    along_z[0][0] = inverse_triple(rho, s001, s002, uz)
    along_z[1][0] = inverse_triple(s100, s101, None, uz)
    along_z[0][1] = inverse_triple(s010, s011, None, uz)
    along_z[2][0] = inverse_triple(s200, None, s202, uz)
    along_z[0][2] = inverse_triple(s020, None, s022, uz)
    along_z[1][1] = inverse_triple(s110, None, s112, uz)
    along_z[2][1] = inverse_triple(None, s211, None, uz)
    along_z[1][2] = inverse_triple(None, s121, None, uz)
    along_z[2][2] = inverse_triple(s220, None, s222, uz)
    out = [None] * 27
    for c in range(3):
        along_y = [
            inverse_triple(along_z[a][0][c], along_z[a][1][c], along_z[a][2][c], uy)
            for a in range(3)
        ]
        for b in range(3):
            triple = inverse_triple(along_y[0][b], along_y[1][b], along_y[2][b], ux)
            for a in range(3):
                out[9 * a + 3 * b + c] = triple[a]
    return out


def turn(value, shift):
    return pltpu.roll(value, shift % 128, axis=1) if shift % 128 else value


def number(cx, cy, cz):
    return 9 * (cx + 1) + 3 * (cy + 1) + cz + 1


def kernel(count_x, count_y, f_hbm, m_hbm, out, f, mask, post, rim, fringe, fringe_mask, halo,
           y_out, y_in, d_in, e_out, e_in,
           in_sem, x_send, x_recv, e_send, e_recv, y_send, y_recv):
    gx, gy = lax.axis_index("gx"), lax.axis_index("gy")
    depth = mask.shape[1]
    tiles = depth // 8

    def device(dx, dy):
        return (lax.rem(gx + dx + count_x, count_x), lax.rem(gy + dy + count_y, count_y))

    barrier = pltpu.get_barrier_semaphore()
    for dx, dy in NEIGHBOURS:
        pl.semaphore_signal(barrier, inc=1, device_id=device(dx, dy), device_id_type=MESH)
    loads = [
        pltpu.make_async_copy(f_hbm, f, in_sem.at[0]),
        pltpu.make_async_copy(m_hbm, mask, in_sem.at[1]),
    ]
    for copy in loads:
        copy.start()

    lane = lax.broadcasted_iota(jnp.int32, (8, 128), 1)
    line = lax.broadcasted_iota(jnp.int32, (8, 128), 0)
    column = lane % 8
    plane = (lane // 8) % 4

    def among(lanes, planes):
        low, high = lanes[0], lanes[-1]
        here = (column >= low) & (column <= high) if low < high else column == low
        one = plane == planes[0]
        for other in planes[1:]:
            one = one | (plane == other)
        return here & one

    def x_copy(s, up):
        lo = 18 if up else 0
        here, there = (2, 0) if up else (1, 3)
        return pltpu.make_async_remote_copy(
            src_ref=post.at[s, pl.ds(lo, NINE), here, pl.ds(PAD, depth)],
            dst_ref=post.at[s, pl.ds(lo, NINE), there, pl.ds(PAD, depth)],
            send_sem=x_send.at[s, up],
            recv_sem=x_recv.at[s, up],
            device_id=device(1 if up else -1, 0),
            device_id_type=MESH,
        )

    def e_copy(s, up):
        return pltpu.make_async_remote_copy(
            src_ref=e_out.at[s, up],
            dst_ref=e_in.at[s, up],
            send_sem=e_send.at[s, up],
            recv_sem=e_recv.at[s, up],
            device_id=device(1 if up else -1, 0),
            device_id_type=MESH,
        )

    def y_copy(up, dx):
        if dx:
            src, dst = y_out.at[up, pl.ds(3 if dx > 0 else 0, 2)], d_in.at[up, (1 - dx) // 2]
        else:
            src, dst = y_out.at[up], y_in.at[up]
        return pltpu.make_async_remote_copy(
            src_ref=src,
            dst_ref=dst,
            send_sem=y_send.at[up, dx + 1],
            recv_sem=y_recv.at[up, 1 - dx],
            device_id=device(dx, 1 if up else -1),
            device_id_type=MESH,
        )

    def relax(s):
        def body(j, carry):
            row = pl.multiple_of(8 * j, 8)
            again = jnp.where(j == 0, PAD + depth, jnp.where(j == tiles - 1, 0, PAD + row))
            again = pl.multiple_of(again, 8)
            for p in (0, 1):
                pops = [f[index, p, pl.ds(row, 8), :] for index in range(27)]
                fluid = mask[p, pl.ds(row, 8), :] == 1
                after = collide(pops)
                for index in range(27):
                    value = jnp.where(fluid, after[index], pops[26 - index])
                    post[s, index, p + 1, pl.ds(PAD + row, 8), :] = value
                    post[s, index, p + 1, pl.ds(again, 8), :] = value
            return carry

        lax.fori_loop(0, tiles, body, 0)

    def make_rim():
        def gather(tile):
            packed = None
            for j in range(tiles):
                for p in (0, 1):
                    start = 32 * j + 8 * (p + 1)
                    value = turn(tile(j, p), start - 125)
                    here = (lane >= start) & (lane < start + 8)
                    packed = value if packed is None else jnp.where(here, value, packed)
            return packed

        def body(third, carry):
            for k in range(3):
                index = 3 * third + k
                rim[index] = gather(lambda j, p: post[0, index, p + 1, PAD + 8 * j : PAD + 8 * j + 8, :])
            return carry

        lax.fori_loop(0, NINE, body, 0)
        rim[MASK] = gather(lambda j, p: mask[p, 8 * j : 8 * j + 8, :].astype(jnp.float32))

    def own_part(index, cy):
        value = None
        for shift, lanes in OWN[cy]:
            moved = turn(rim[index], shift)
            value = moved if value is None else jnp.where(among(lanes, (1, 2)), moved, value)
        return value

    def slot(t):
        return t // 2, 16 * (t % 2), (3, 0) if t % 2 else (1, 2)

    def make_messages():
        for up in (0, 1):
            packed = [jnp.zeros((8, 128), jnp.float32)] * 5
            for t in range(10):
                tile, extra, planes = slot(t)
                for cy in (-1, 0, 1):
                    if t == NINE and cy:
                        continue
                    index = MASK if t == NINE else number(t // 3 - 1, cy, t % 3 - 1)
                    shift, lanes, _, _ = SENT[up][cy]
                    value = turn(rim[index], shift + extra)
                    packed[tile] = jnp.where(among(lanes, planes), value, packed[tile])
            for tile in range(5):
                y_out[up, tile] = packed[tile]

    def from_side(ref, first, t, cy, up, across, planes, value):
        tile, extra, _ = slot(t)
        _, _, shift, lanes = SENT[up][cy]
        moved = turn(ref[tile - first], shift - extra + across)
        return jnp.where(among(lanes, planes), moved, value)

    def send_fringe(s):
        for up in (0, 1):
            for tile in range(3):
                packed = None
                for q in range(4 * tile, min(4 * tile + 4, NINE)):
                    value = turn(fringe[18 * up + q], 8 * (q % 4 - 1 - up))
                    packed = value if packed is None else jnp.where(plane == q % 4, value, packed)
                e_out[s, up, tile] = packed
            e_copy(s, up).start()

    def receive_fringe(s):
        for up in (0, 1):
            e_copy(s, up).wait_recv()
            there = 0 if up else 3
            for q in range(NINE):
                index = 18 * up + q
                moved = turn(e_in[s, up, q // 4], 8 * (there - q % 4))
                fringe[index] = jnp.where(plane == there, moved, fringe[index])

    def receive_sides():
        for up in (0, 1):
            for dx in (-1, 0, 1):
                y_copy(up, dx).wait_recv()
        for t in range(NINE):
            cx = t // 3 - 1
            for cy in (-1, 0, 1):
                index = number(cx, cy, t % 3 - 1)
                value = fringe[index]
                for up in (0, 1):
                    value = from_side(y_in.at[up], 0, t, cy, up, 0, (1, 2), value)
                    if cx:
                        near = d_in.at[up, 0 if cx > 0 else 1]
                        first, there = (3, 0) if cx > 0 else (0, 3)
                        value = from_side(near, first, t, cy, up, -16 * cx, (there,), value)
                fringe[index] = value
        value = own_part(MASK, 0)
        for up in (0, 1):
            value = from_side(y_in.at[up], 0, NINE, 0, up, 0, (1, 2), value)
        fringe_mask[...] = value

    def lay_out():
        by_cx = []
        for cx in (-1, 0, 1):
            value = None
            for cz in (-1, 0, 1):
                for cy in (1, -1):
                    target = 2 * (cz + 1) + (1 if cy > 0 else 0)
                    moved = turn(fringe[number(cx, cy, cz)], target - (2 if cy > 0 else 4))
                    value = moved if value is None else jnp.where(column == target, moved, value)
            by_cx.append(value)
        block = lane // 32
        for j in range(tiles):
            parts = [turn(by_cx[b], 32 * (b - j)) for b in range(3)]
            rows = jnp.where(block == 0, parts[0], jnp.where(block == 1, parts[1], parts[2]))
            halo[PAD + 8 * j : PAD + 8 * j + 8, :] = rows
            if j == 0:
                halo[PAD + depth : PAD + depth + 8, :] = rows
            if j == tiles - 1:
                halo[0:8, :] = rows

    def step_fringe():
        pops = []
        for index in range(27):
            cx, cz = index // 9 - 1, index % 3 - 1
            value = turn(fringe[index], 8 * cx)
            if cz:
                value = pltpu.roll(value, cz % 8, axis=0)
                value = jnp.where(line == (0 if cz > 0 else 7), turn(value, 32 * cz), value)
            pops.append(value)
        after = collide(pops)
        fluid = fringe_mask[...] == 1.0
        for index in range(27):
            value = jnp.where(fluid, after[index], pops[26 - index])
            fringe[index] = turn(value, index // 3 % 3 - 1)

    def ends(row, p, cx, cz):
        place = 32 * (cx + 1) + 8 * (p + 1 - cx) + 2 * (cz + 1) + 1
        return pltpu.roll(halo[pl.ds(PAD + row - cz, 8), :], (-place) % 128, axis=1)

    def place_own(s, to):
        def body(j, carry):
            row = pl.multiple_of(8 * j, 8)
            for p in (0, 1):
                for cx in (0, 2 * p - 1):
                    for cy in (-1, 0, 1):
                        for cz in (-1, 0, 1):
                            index = 9 * (cx + 1) + 3 * (cy + 1) + cz + 1
                            value = post[s, index, p + 1 - cx, pl.ds(PAD + row - cz, 8), :]
                            if cy:
                                value = pltpu.roll(value, cy % 128, axis=1)
                            to[index, p, pl.ds(row, 8), :] = value
            return carry

        lax.fori_loop(0, tiles, body, 0)

    def place_edges(to):
        def body(j, carry):
            row = pl.multiple_of(8 * j, 8)
            for p in (0, 1):
                for cx in (0, 2 * p - 1):
                    for cz in (-1, 0, 1):
                        both = ends(row, p, cx, cz)
                        for cy in (-1, 1):
                            index = 9 * (cx + 1) + 3 * (cy + 1) + cz + 1
                            value = to[index, p, pl.ds(row, 8), :]
                            end = 0 if cy > 0 else 127
                            to[index, p, pl.ds(row, 8), :] = jnp.where(lane == end, both, value)
            return carry

        lax.fori_loop(0, tiles, body, 0)

    def place_faces(s, to):
        for there, lo in ((0, 18), (3, 0)):
            for index in range(lo, lo + NINE):
                post[s, index, there, 0:8, :] = post[s, index, there, depth : depth + 8, :]
                post[s, index, there, PAD + depth : PAD + depth + 8, :] = post[
                    s, index, there, PAD : PAD + 8, :
                ]

        def body(j, carry):
            row = pl.multiple_of(8 * j, 8)
            for p in (0, 1):
                cx = 1 - 2 * p
                for cz in (-1, 0, 1):
                    both = ends(row, p, cx, cz)
                    for cy in (-1, 0, 1):
                        index = 9 * (cx + 1) + 3 * (cy + 1) + cz + 1
                        value = post[s, index, p + 1 - cx, pl.ds(PAD + row - cz, 8), :]
                        if cy:
                            value = pltpu.roll(value, cy % 128, axis=1)
                            end = 0 if cy > 0 else 127
                            value = jnp.where(lane == end, both, value)
                        to[index, p, pl.ds(row, 8), :] = value
            return carry

        lax.fori_loop(0, tiles, body, 0)

    for copy in loads:
        copy.wait()
    relax(0)
    make_rim()
    make_messages()
    for index in range(27):
        fringe[index] = own_part(index, index // 3 % 3 - 1)
    pl.semaphore_wait(barrier, len(NEIGHBOURS))
    for up in (0, 1):
        for dx in (0, -1, 1):
            y_copy(up, dx).start()
    send_fringe(0)
    for s in range(STEPS):
        last = s == STEPS - 1
        to = out if last else f
        for up in (0, 1):
            x_copy(s, up).start()
        place_own(s, to)
        receive_fringe(s)
        if s == 0:
            receive_sides()
        lay_out()
        if not last:
            step_fringe()
            send_fringe(s + 1)
        place_edges(to)
        for up in (0, 1):
            x_copy(s, up).wait_recv()
        place_faces(s, to)
        if not last:
            relax(s + 1)
    for up in (0, 1):
        for dx in (-1, 0, 1):
            y_copy(up, dx).wait_send()
        for s in range(STEPS):
            x_copy(s, up).wait_send()
            e_copy(s, up).wait_send()


def solution(mesh):
    count_x, count_y = mesh.shape["gx"], mesh.shape["gy"]

    def on_device(populations, fluid_mask):
        width_x, depth, width_y = fluid_mask.shape
        tall = depth + 2 * PAD

        def body(*refs):
            kernel(count_x, count_y, *refs)

        return pl.pallas_call(
            body,
            out_shape=pltpu.VMEM(populations.shape, jnp.float32),
            in_specs=[pl.BlockSpec(memory_space=pltpu.HBM)] * 2,
            out_specs=pl.BlockSpec(memory_space=pltpu.VMEM),
            scratch_shapes=[
                pltpu.VMEM(populations.shape, jnp.float32),
                pltpu.VMEM(fluid_mask.shape, jnp.int32),
                pltpu.VMEM((STEPS, 27, width_x + 2, tall, width_y), jnp.float32),
                pltpu.VMEM((MASK + 1, 8, 128), jnp.float32),
                pltpu.VMEM((27, 8, 128), jnp.float32),
                pltpu.VMEM((8, 128), jnp.float32),
                pltpu.VMEM((tall, 128), jnp.float32),
                pltpu.VMEM((2, 5, 8, 128), jnp.float32),
                pltpu.VMEM((2, 5, 8, 128), jnp.float32),
                pltpu.VMEM((2, 2, 2, 8, 128), jnp.float32),
                pltpu.VMEM((STEPS, 2, 3, 8, 128), jnp.float32),
                pltpu.VMEM((STEPS, 2, 3, 8, 128), jnp.float32),
                pltpu.SemaphoreType.DMA((2,)),
                pltpu.SemaphoreType.DMA((STEPS, 2)),
                pltpu.SemaphoreType.DMA((STEPS, 2)),
                pltpu.SemaphoreType.DMA((STEPS, 2)),
                pltpu.SemaphoreType.DMA((STEPS, 2)),
                pltpu.SemaphoreType.DMA((2, 3)),
                pltpu.SemaphoreType.DMA((2, 3)),
            ],
            compiler_params=pltpu.CompilerParams(
                collective_id=0, has_side_effects=True, vmem_limit_bytes=60 * 2**20
            ),
            cost_estimate=pl.CostEstimate(
                flops=500 * STEPS * fluid_mask.size,
                bytes_accessed=8 * populations.size,
                transcendentals=0,
            ),
            name="lattice_steps",
        )(populations, fluid_mask)

    in_specs = (P(None, "gx", None, "gy"), P("gx", None, "gy"))
    out_specs = P(None, "gx", None, "gy")
    return jax.shard_map(
        on_device, mesh=mesh, in_specs=in_specs, out_specs=out_specs, check_vma=False
    )
```

time: 45.9 us -> 35.7 us (0.78)
  Pallas kernels: 42.9 us -> 34.7 us
  local copies, waits for them, and re-layouts: 2.84 us -> 0.91 us
    pallas_call x1, Pallas kernels: 42.9 us -> 34.7 us  [on_device(): pl.pallas_call(body, out_shape=pltpu.VMEM(populations.shape, jnp.float32)...]
    unnamed x5 -> x1, local copies, waits for them, and re-layouts: 2.84 us -> 0.91 us
where the time goes in v2:
time: 35.7 us; the launch traced here: 35.6 us
  Pallas kernels  34.7 us (97%)
  local copies, waits for them, and re-layouts  0.91 us (3%)
    pallas_call x1, Pallas kernels, on_device(): pl.pallas_call(body, out_shape=pltpu.VMEM(populations.shape, jnp.float32)...  34.7 us
    unnamed x1, local copies, waits for them, and re-layouts  0.91 us

profile of v2, /device:TPU:1, one launch (start us, length us, event | category | flops | bytes accessed | tf_op | source)
XLA Modules:
  0.0 35.6 jit_solution(10158593082599611133)
XLA Ops:
  0.0 34.7 %lattice_steps.1 = f32[27,2,32,128]{3,2,1,0:T(8,128)S(1)} custom-call(f32[27,2,32,128]{3,2,1,0:T(8,128)} %refs_0_.1, s32[2,32,128]{2,1,0:T(8,128)} %refs_1_.1), custom_call_target="tpu_custom_call" | custom-call | flops 12288000 | bytes 1769472 | tf_op jit(solution)/shard_map/lattice_steps/pallas_call | solution.py:456
  34.7 0.9 %copy.4 = f32[27,2,32,128]{3,2,1,0:T(8,128)} copy(f32[27,2,32,128]{3,2,1,0:T(8,128)S(1)} %lattice_steps.1) | data formatting | bytes 1769472

commit v3 on v2

--- a/solution.py
+++ b/solution.py
@@ -17,10 +17,10 @@
 NINE = 9
 NEIGHBOURS = [(dx, dy) for dx in (-1, 0, 1) for dy in (-1, 0, 1) if dx or dy]
 
-OWN = {1: [(3, (4, 5))], 0: [(-1, (2,)), (2, (4,))], -1: [(-2, (1, 2))]}
+OWN = {1: [(0, (3,)), (4, (4, 5, 6))], 0: [(-1, (2, 3)), (3, (4, 5))], -1: [(-2, (1, 2, 3)), (2, (4,))]}
 SENT = {
     1: {1: (0, (0, 1, 2), 0, (0, 1, 2)), 0: (2, (3, 4), -3, (0, 1)), -1: (3, (5,), -5, (0,))},
-    0: {-1: (-3, (0, 1, 2), 4, (4, 5, 6)), 0: (0, (3, 4), 2, (5, 6)), 1: (2, (5,), 1, (6,))},
+    0: {-1: (-3, (0, 1, 2), 5, (5, 6, 7)), 0: (0, (3, 4), 3, (6, 7)), 1: (2, (5,), 2, (7,))},
 }
 MASK = 27
 
@@ -134,7 +134,7 @@
            y_out, y_in, d_in, e_out, e_in,
            in_sem, x_send, x_recv, e_send, e_recv, y_send, y_recv):
     gx, gy = lax.axis_index("gx"), lax.axis_index("gy")
-    depth = mask.shape[1]
+    depth = post.shape[3] - 2 * PAD
     tiles = depth // 8
 
     def device(dx, dy):
@@ -145,7 +145,7 @@
         pl.semaphore_signal(barrier, inc=1, device_id=device(dx, dy), device_id_type=MESH)
     loads = [
         pltpu.make_async_copy(f_hbm, f, in_sem.at[0]),
-        pltpu.make_async_copy(m_hbm, mask, in_sem.at[1]),
+        pltpu.make_async_copy(m_hbm, mask.at[:, pl.ds(0, depth)], in_sem.at[1]),
     ]
     for copy in loads:
         copy.start()
@@ -163,14 +163,15 @@
             one = one | (plane == other)
         return here & one
 
-    def x_copy(s, up):
+    def x_copy(s, up, j):
+        rows = pl.ds(PAD + 8 * j, 8)
         lo = 18 if up else 0
         here, there = (2, 0) if up else (1, 3)
         return pltpu.make_async_remote_copy(
-            src_ref=post.at[s, pl.ds(lo, NINE), here, pl.ds(PAD, depth)],
-            dst_ref=post.at[s, pl.ds(lo, NINE), there, pl.ds(PAD, depth)],
-            send_sem=x_send.at[s, up],
-            recv_sem=x_recv.at[s, up],
+            src_ref=post.at[s, pl.ds(lo, NINE), here, rows],
+            dst_ref=post.at[s, pl.ds(lo, NINE), there, rows],
+            send_sem=x_send.at[s, up, j],
+            recv_sem=x_recv.at[s, up, j],
             device_id=device(1 if up else -1, 0),
             device_id_type=MESH,
         )
@@ -199,22 +200,59 @@
             device_id_type=MESH,
         )
 
+    def shift_of(s):
+        return 1 if s < STEPS - 1 else 1 - STEPS
+
+    def streamed(s, p, cx, row):
+        pops = {}
+        for cz in (-1, 0, 1):
+            for cy in (-1, 0, 1):
+                value = post[s, number(cx, cy, cz), p + 1 - cx, pl.ds(PAD + row + shift_of(s) - cz, 8), :]
+                if cy:
+                    value = pltpu.roll(value, cy % 128, axis=1)
+                pops[number(cx, cy, cz)] = value
+            with_ends(s, row, p, cx, cz, pops)
+        return pops
+
     def relax(s):
         def body(j, carry):
             row = pl.multiple_of(8 * j, 8)
             again = jnp.where(j == 0, PAD + depth, jnp.where(j == tiles - 1, 0, PAD + row))
             again = pl.multiple_of(again, 8)
+            if s:
+
+                @pl.when(j < tiles - 1)
+                def _():
+                    for up in (0, 1):
+                        x_copy(s - 1, up, j + 1).wait_recv()
+
             for p in (0, 1):
-                pops = [f[index, p, pl.ds(row, 8), :] for index in range(27)]
-                fluid = mask[p, pl.ds(row, 8), :] == 1
+                far = streamed(s - 1, p, 1 - 2 * p, row) if s else {}
+                pops = [
+                    far[index] if index in far else f[index, p, pl.ds(row, 8), :]
+                    for index in range(27)
+                ]
+                fluid = mask[p, pl.ds(row + s, 8), :] == 1
                 after = collide(pops)
                 for index in range(27):
                     value = jnp.where(fluid, after[index], pops[26 - index])
                     post[s, index, p + 1, pl.ds(PAD + row, 8), :] = value
                     post[s, index, p + 1, pl.ds(again, 8), :] = value
+            if s:
+                for up in (0, 1):
+                    x_copy(s, up, j).start()
             return carry
 
+        if s:
+            for up in (0, 1):
+                x_copy(s - 1, up, 0).wait_recv()
+            wrap_faces(s - 1, PAD, PAD + depth)
         lax.fori_loop(0, tiles, body, 0)
+
+    def wrap_faces(s, start, end):
+        for there, lo in ((0, 18), (3, 0)):
+            for index in range(lo, lo + NINE):
+                post[s, index, there, end : end + 8, :] = post[s, index, there, start : start + 8, :]
 
     def make_rim():
         def gather(tile):
@@ -307,25 +345,26 @@
             value = from_side(y_in.at[up], 0, NINE, 0, up, 0, (1, 2), value)
         fringe_mask[...] = value
 
-    def lay_out():
-        by_cx = []
-        for cx in (-1, 0, 1):
-            value = None
-            for cz in (-1, 0, 1):
-                for cy in (1, -1):
-                    target = 2 * (cz + 1) + (1 if cy > 0 else 0)
-                    moved = turn(fringe[number(cx, cy, cz)], target - (2 if cy > 0 else 4))
-                    value = moved if value is None else jnp.where(column == target, moved, value)
-            by_cx.append(value)
+    def lay_out(s):
         block = lane // 32
-        for j in range(tiles):
-            parts = [turn(by_cx[b], 32 * (b - j)) for b in range(3)]
-            rows = jnp.where(block == 0, parts[0], jnp.where(block == 1, parts[1], parts[2]))
-            halo[PAD + 8 * j : PAD + 8 * j + 8, :] = rows
-            if j == 0:
-                halo[PAD + depth : PAD + depth + 8, :] = rows
-            if j == tiles - 1:
-                halo[0:8, :] = rows
+        for cz in (-1, 0, 1):
+            by_cx = []
+            for cx in (-1, 0, 1):
+                value = fringe[number(cx, 1, cz)]
+                value = jnp.where(column < 2, turn(fringe[number(cx, -1, cz)], -4), value)
+                if s == STEPS - 1:
+                    rest = fringe[number(cx, 0, cz)]
+                    value = jnp.where(column == 4, turn(rest, -1), value)
+                    value = jnp.where(column == 5, turn(rest, 3), value)
+                by_cx.append(value)
+            for j in range(tiles):
+                parts = [turn(by_cx[b], 32 * (b - j)) for b in range(3)]
+                rows = jnp.where(block == 0, parts[0], jnp.where(block == 1, parts[1], parts[2]))
+                halo[cz + 1, PAD + 8 * j : PAD + 8 * j + 8, :] = rows
+                if j == 0:
+                    halo[cz + 1, PAD + depth : PAD + depth + 8, :] = rows
+                if j == tiles - 1:
+                    halo[cz + 1, 0:8, :] = rows
 
     def step_fringe():
         pops = []
@@ -342,9 +381,19 @@
             value = jnp.where(fluid, after[index], pops[26 - index])
             fringe[index] = turn(value, index // 3 % 3 - 1)
 
-    def ends(row, p, cx, cz):
-        place = 32 * (cx + 1) + 8 * (p + 1 - cx) + 2 * (cz + 1) + 1
-        return pltpu.roll(halo[pl.ds(PAD + row - cz, 8), :], (-place) % 128, axis=1)
+    def with_ends(s, row, p, cx, cz, pops):
+        if s == 0:
+            return
+        rows = halo[cz + 1, pl.ds(PAD + row + shift_of(s) + s - cz, 8), :]
+        place = 32 * (cx + 1) + 8 * (p + 1 - cx)
+        both = pltpu.roll(rows, (-place - 2) % 128, axis=1)
+        low, high = number(cx, -1, cz), number(cx, 1, cz)
+        pops[high] = jnp.where(lane < 2, both, pops[high])
+        pops[low] = jnp.where(lane >= 126, both, pops[low])
+        if s == STEPS - 1:
+            both = pltpu.roll(rows, (-place - 5) % 128, axis=1)
+            rest = number(cx, 0, cz)
+            pops[rest] = jnp.where((lane == 0) | (lane == 127), both, pops[rest])
 
     def place_own(s, to):
         def body(j, carry):
@@ -353,8 +402,9 @@
                 for cx in (0, 2 * p - 1):
                     for cy in (-1, 0, 1):
                         for cz in (-1, 0, 1):
-                            index = 9 * (cx + 1) + 3 * (cy + 1) + cz + 1
-                            value = post[s, index, p + 1 - cx, pl.ds(PAD + row - cz, 8), :]
+                            index = number(cx, cy, cz)
+                            start = PAD + row + shift_of(s) - cz
+                            value = post[s, index, p + 1 - cx, pl.ds(start, 8), :]
                             if cy:
                                 value = pltpu.roll(value, cy % 128, axis=1)
                             to[index, p, pl.ds(row, 8), :] = value
@@ -362,50 +412,38 @@
 
         lax.fori_loop(0, tiles, body, 0)
 
-    def place_edges(to):
+    def place_ends(s, to):
         def body(j, carry):
             row = pl.multiple_of(8 * j, 8)
             for p in (0, 1):
                 for cx in (0, 2 * p - 1):
                     for cz in (-1, 0, 1):
-                        both = ends(row, p, cx, cz)
-                        for cy in (-1, 1):
-                            index = 9 * (cx + 1) + 3 * (cy + 1) + cz + 1
-                            value = to[index, p, pl.ds(row, 8), :]
-                            end = 0 if cy > 0 else 127
-                            to[index, p, pl.ds(row, 8), :] = jnp.where(lane == end, both, value)
+                        names = [number(cx, cy, cz) for cy in ((-1, 0, 1) if s == STEPS - 1 else (-1, 1))]
+                        pops = {index: to[index, p, pl.ds(row, 8), :] for index in names}
+                        with_ends(s, row, p, cx, cz, pops)
+                        for index in names:
+                            to[index, p, pl.ds(row, 8), :] = pops[index]
             return carry
 
         lax.fori_loop(0, tiles, body, 0)
 
     def place_faces(s, to):
-        for there, lo in ((0, 18), (3, 0)):
-            for index in range(lo, lo + NINE):
-                post[s, index, there, 0:8, :] = post[s, index, there, depth : depth + 8, :]
-                post[s, index, there, PAD + depth : PAD + depth + 8, :] = post[
-                    s, index, there, PAD : PAD + 8, :
-                ]
-
-        def body(j, carry):
-            row = pl.multiple_of(8 * j, 8)
+        for up in (0, 1):
+            x_copy(s, up, 0).wait_recv()
+        for j in range(1, tiles + 1):
+            if j < tiles:
+                for up in (0, 1):
+                    x_copy(s, up, j).wait_recv()
+            else:
+                wrap_faces(s, depth, 0)
+            row = 8 * (j % tiles)
             for p in (0, 1):
-                cx = 1 - 2 * p
-                for cz in (-1, 0, 1):
-                    both = ends(row, p, cx, cz)
-                    for cy in (-1, 0, 1):
-                        index = 9 * (cx + 1) + 3 * (cy + 1) + cz + 1
-                        value = post[s, index, p + 1 - cx, pl.ds(PAD + row - cz, 8), :]
-                        if cy:
-                            value = pltpu.roll(value, cy % 128, axis=1)
-                            end = 0 if cy > 0 else 127
-                            value = jnp.where(lane == end, both, value)
-                        to[index, p, pl.ds(row, 8), :] = value
-            return carry
-
-        lax.fori_loop(0, tiles, body, 0)
+                for index, value in streamed(s, p, 1 - 2 * p, row).items():
+                    to[index, p, row : row + 8, :] = value
 
     for copy in loads:
         copy.wait()
+    mask[:, depth : depth + 8, :] = mask[:, 0:8, :]
     relax(0)
     make_rim()
     make_messages()
@@ -416,31 +454,34 @@
         for dx in (0, -1, 1):
             y_copy(up, dx).start()
     send_fringe(0)
-    for s in range(STEPS):
-        last = s == STEPS - 1
-        to = out if last else f
-        for up in (0, 1):
-            x_copy(s, up).start()
-        place_own(s, to)
-        receive_fringe(s)
-        if s == 0:
-            receive_sides()
-        lay_out()
-        if not last:
-            step_fringe()
-            send_fringe(s + 1)
-        place_edges(to)
-        for up in (0, 1):
-            x_copy(s, up).wait_recv()
-        place_faces(s, to)
-        if not last:
-            relax(s + 1)
+    for j in range(tiles):
+        for up in (0, 1):
+            x_copy(0, up, j).start()
+    place_own(0, f)
+    relax(1)
+    place_own(1, f)
+    receive_fringe(0)
+    receive_sides()
+    step_fringe()
+    send_fringe(1)
+    receive_fringe(1)
+    lay_out(1)
+    step_fringe()
+    send_fringe(2)
+    place_ends(1, f)
+    relax(2)
+    place_own(2, out)
+    receive_fringe(2)
+    lay_out(2)
+    place_ends(2, out)
+    place_faces(2, out)
     for up in (0, 1):
         for dx in (-1, 0, 1):
             y_copy(up, dx).wait_send()
         for s in range(STEPS):
-            x_copy(s, up).wait_send()
             e_copy(s, up).wait_send()
+            for j in range(tiles):
+                x_copy(s, up, j).wait_send()
 
 
 def solution(mesh):
@@ -460,20 +501,20 @@
             out_specs=pl.BlockSpec(memory_space=pltpu.VMEM),
             scratch_shapes=[
                 pltpu.VMEM(populations.shape, jnp.float32),
-                pltpu.VMEM(fluid_mask.shape, jnp.int32),
+                pltpu.VMEM((width_x, depth + 8, width_y), jnp.int32),
                 pltpu.VMEM((STEPS, 27, width_x + 2, tall, width_y), jnp.float32),
                 pltpu.VMEM((MASK + 1, 8, 128), jnp.float32),
                 pltpu.VMEM((27, 8, 128), jnp.float32),
                 pltpu.VMEM((8, 128), jnp.float32),
-                pltpu.VMEM((tall, 128), jnp.float32),
+                pltpu.VMEM((3, tall, 128), jnp.float32),
                 pltpu.VMEM((2, 5, 8, 128), jnp.float32),
                 pltpu.VMEM((2, 5, 8, 128), jnp.float32),
                 pltpu.VMEM((2, 2, 2, 8, 128), jnp.float32),
                 pltpu.VMEM((STEPS, 2, 3, 8, 128), jnp.float32),
                 pltpu.VMEM((STEPS, 2, 3, 8, 128), jnp.float32),
                 pltpu.SemaphoreType.DMA((2,)),
-                pltpu.SemaphoreType.DMA((STEPS, 2)),
-                pltpu.SemaphoreType.DMA((STEPS, 2)),
+                pltpu.SemaphoreType.DMA((STEPS, 2, depth // 8)),
+                pltpu.SemaphoreType.DMA((STEPS, 2, depth // 8)),
                 pltpu.SemaphoreType.DMA((STEPS, 2)),
                 pltpu.SemaphoreType.DMA((STEPS, 2)),
                 pltpu.SemaphoreType.DMA((2, 3)),

time: 35.7 us -> 34.1 us (0.955)
  Pallas kernels: 34.7 us -> 33 us
    pallas_call x1, Pallas kernels: 34.7 us -> 33 us  [on_device(): pl.pallas_call(body, out_shape=pltpu.VMEM(populations.shape, jnp.float32)...]
where the time goes in v3:
time: 34.1 us; the launch traced here: 33.9 us
  Pallas kernels  33 us (97%)
  local copies, waits for them, and re-layouts  0.91 us (3%)
    pallas_call x1, Pallas kernels, on_device(): pl.pallas_call(body, out_shape=pltpu.VMEM(populations.shape, jnp.float32)...  33 us
    unnamed x1, local copies, waits for them, and re-layouts  0.91 us

profile of v3, /device:TPU:1, one launch (start us, length us, event | category | flops | bytes accessed | tf_op | source)
XLA Modules:
  0.0 33.9 jit_solution(13642175043499808295)
XLA Ops:
  0.0 33.0 %lattice_steps.1 = f32[27,2,32,128]{3,2,1,0:T(8,128)S(1)} custom-call(f32[27,2,32,128]{3,2,1,0:T(8,128)} %refs_0_.1, s32[2,32,128]{2,1,0:T(8,128)} %refs_1_.1), custom_call_target="tpu_custom_call" | custom-call | flops 12288000 | bytes 1769472 | tf_op jit(solution)/shard_map/lattice_steps/pallas_call | solution.py:497
  33.0 0.9 %copy.4 = f32[27,2,32,128]{3,2,1,0:T(8,128)} copy(f32[27,2,32,128]{3,2,1,0:T(8,128)S(1)} %lattice_steps.1) | data formatting | bytes 1769472

commit v4 on v3

v4 whole, which is shorter than its diff:
```python
import jax
import jax.numpy as jnp
from jax import lax
from jax.experimental import pallas as pl
from jax.experimental.pallas import tpu as pltpu
from jax.sharding import PartitionSpec as P

STEPS = 3
MESH = pl.DeviceIdType.MESH

shear_rate = 1.6
body_force = 0.002
keep = 1.0 - shear_rate
third = 1.0 / 3.0

PAD = 8
NINE = 9
ALONG_X = [(-1, 0), (1, 0)]
ACROSS = [(dx, dy) for dx in (-1, 0, 1) for dy in (-1, 1)]

OWN = {cy: [(cy - 4, (2 + cy, 6)), (7 + cy, (8, 12 + cy))] for cy in (-1, 0, 1)}
SENT = {
    1: {1: (-3, (0, 2), 0, (0, 2)), 0: (-1, (3, 4), -3, (0, 1)), -1: (0, (5, 5), -5, (0, 0))},
    0: {-1: (-6, (0, 2), 12, (12, 14)), 0: (-3, (3, 4), 10, (13, 14)), 1: (-1, (5, 5), 9, (14, 14))},
}
SLOTS = {(-1, -1): (0, 0), (-1, 0): (0, 1), (-1, 1): (0, 2), (0, -1): (0, 3),
         (1, -1): (1, 0), (1, 0): (1, 1), (1, 1): (1, 2), (0, 0): (1, 3),
         (0, 1): (2, 0), None: (2, 1)}
MASK = 27


def inverse_triple(zeroth, first, second, speed):
    if zeroth is None:
        raw_one = first
        raw_two = 2.0 * speed * first
        rest = -raw_two
    else:
        if first is None:
            raw_one = speed * zeroth
            raw_two = second + speed * raw_one
        else:
            raw_one = first + speed * zeroth
            raw_two = speed * (first + raw_one)
            if second is not None:
                raw_two = second + raw_two
        rest = zeroth - raw_two
    plus = 0.5 * (raw_two + raw_one)
    return plus - raw_one, rest, plus


def collide(f):
    g = [[[f[9 * a + 3 * b + c] for c in range(3)] for b in range(3)] for a in range(3)]
    even = [[g[2][b][c] + g[0][b][c] for c in range(3)] for b in range(3)]
    diff = [[g[2][b][c] - g[0][b][c] for c in range(3)] for b in range(3)]
    total = [[even[b][c] + g[1][b][c] for c in range(3)] for b in range(3)]
    t_even = [total[2][c] + total[0][c] for c in range(3)]
    t_diff = [total[2][c] - total[0][c] for c in range(3)]
    t_total = [t_even[c] + total[1][c] for c in range(3)]
    d_total = [diff[2][c] + diff[0][c] + diff[1][c] for c in range(3)]
    d_diff = [diff[2][c] - diff[0][c] for c in range(3)]
    e_total = [even[2][c] + even[0][c] + even[1][c] for c in range(3)]
    m002 = t_total[2] + t_total[0]
    jz = t_total[2] - t_total[0]
    rho = m002 + t_total[1]
    jy = t_diff[0] + t_diff[1] + t_diff[2]
    m011 = t_diff[2] - t_diff[0]
    m020 = t_even[0] + t_even[1] + t_even[2]
    jx = d_total[0] + d_total[1] + d_total[2]
    m101 = d_total[2] - d_total[0]
    m110 = d_diff[0] + d_diff[1] + d_diff[2]
    m200 = e_total[0] + e_total[1] + e_total[2]
    r = 1.0 / rho
    ux = (jx + 0.5 * body_force) * r
    uy = jy * r
    uz = jz * r
    s100 = ux * rho - jx
    s010 = uy * rho - jy
    s001 = uz * rho - jz
    k200 = m200 - ux * (jx - s100)
    k020 = m020 - uy * (jy - s010)
    k002 = m002 - uz * (jz - s001)
    k110 = m110 - ux * jy + uy * s100
    k101 = m101 - ux * jz + uz * s100
    k011 = m011 - uy * jz + uz * s010
    base = third * rho - (keep * third) * (k200 + k020 + k002)
    s200 = keep * k200 + base
    s020 = keep * k020 + base
    s002 = keep * k002 + base
    s110 = keep * k110
    s101 = keep * k101
    s011 = keep * k011
    d110 = 2.0 * s110
    d101 = 2.0 * s101
    d011 = 2.0 * s011
    q110 = d110 * s110
    q101 = d101 * s101
    q011 = d011 * s011
    p220 = s200 * s020 + q110
    s220 = p220 * r
    s202 = (s200 * s002 + q101) * r
    s022 = (s020 * s002 + q011) * r
    s211 = (s200 * s011 + d110 * s101) * r
    s121 = (s020 * s101 + d110 * s011) * r
    s112 = (s002 * s110 + d101 * s011) * r
    s222 = (p220 * s002 + q101 * s020 + q011 * s200 + 2.0 * d110 * s101 * d011) * (r * r)
    along_z = [[None] * 3 for _ in range(3)]
    along_z[0][0] = inverse_triple(rho, s001, s002, uz)
    along_z[1][0] = inverse_triple(s100, s101, None, uz)
    along_z[0][1] = inverse_triple(s010, s011, None, uz)
    along_z[2][0] = inverse_triple(s200, None, s202, uz)
    along_z[0][2] = inverse_triple(s020, None, s022, uz)
    along_z[1][1] = inverse_triple(s110, None, s112, uz)
    along_z[2][1] = inverse_triple(None, s211, None, uz)
    along_z[1][2] = inverse_triple(None, s121, None, uz)
    along_z[2][2] = inverse_triple(s220, None, s222, uz)
    out = [None] * 27
    for c in range(3):
        along_y = [
            inverse_triple(along_z[a][0][c], along_z[a][1][c], along_z[a][2][c], uy)
            for a in range(3)
        ]
        for b in range(3):
            triple = inverse_triple(along_y[0][b], along_y[1][b], along_y[2][b], ux)
            for a in range(3):
                out[9 * a + 3 * b + c] = triple[a]
    return out


def turn(value, shift):
    return pltpu.roll(value, shift % 128, axis=1) if shift % 128 else value


def number(cx, cy, cz):
    return 9 * (cx + 1) + 3 * (cy + 1) + cz + 1


def kernel(count_x, count_y, f_hbm, m_hbm, out, f, mask, post, rim, fringe, fringe_mask,
           y_out, y_in, d_in, e_out, e_in,
           ready, in_sem, x_send, x_recv, e_send, e_recv, y_send, y_recv):
    gx, gy = lax.axis_index("gx"), lax.axis_index("gy")
    depth = post.shape[3] - 2 * PAD
    tiles = depth // 8
    half = depth // 2

    def device(dx, dy):
        return (lax.rem(gx + dx + count_x, count_x), lax.rem(gy + dy + count_y, count_y))

    barrier = pltpu.get_barrier_semaphore()
    odd = lax.rem(gy, 2)

    def tell(semaphore, places):
        for dx, dy in places:
            pl.semaphore_signal(semaphore, inc=1, device_id=device(dx, dy), device_id_type=MESH)

    tell(barrier, ALONG_X)

    @pl.when(odd == 0)
    def _():
        tell(barrier, ACROSS)

    def load(j):
        rows = pl.ds(pl.multiple_of(8 * j, 8), 8)
        return pltpu.make_async_copy(f_hbm.at[:, :, rows], f.at[:, :, rows], in_sem.at[j])

    load_mask = pltpu.make_async_copy(m_hbm, mask.at[:, pl.ds(0, depth)], in_sem.at[tiles])
    load_mask.start()
    for j in range(tiles):
        load(j).start()

    lane = lax.broadcasted_iota(jnp.int32, (8, 128), 1)
    line = lax.broadcasted_iota(jnp.int32, (8, 128), 0)
    column = lane % 16
    plane = (lane // 16) % 4

    def among(lanes, planes):
        low, high = lanes
        here = (column >= low) & (column <= high) if low < high else column == low
        one = plane == planes[0]
        for other in planes[1:]:
            one = one | (plane == other)
        return here & one

    def x_copy(s, up, j):
        rows = pl.ds(PAD + half * j, half)
        lo = 18 if up else 0
        here, there = (2, 0) if up else (1, 3)
        return pltpu.make_async_remote_copy(
            src_ref=post.at[s, pl.ds(lo, NINE), here, rows],
            dst_ref=post.at[s, pl.ds(lo, NINE), there, rows],
            send_sem=x_send.at[s, up, j],
            recv_sem=x_recv.at[s, up, j],
            device_id=device(1 if up else -1, 0),
            device_id_type=MESH,
        )

    def e_copy(s, up):
        return pltpu.make_async_remote_copy(
            src_ref=e_out.at[s, up],
            dst_ref=e_in.at[s, up],
            send_sem=e_send.at[s, up],
            recv_sem=e_recv.at[s, up],
            device_id=device(1 if up else -1, 0),
            device_id_type=MESH,
        )

    def y_copy(up, dx):
        if dx:
            src, dst = y_out.at[up, (1 + dx) // 2], d_in.at[up, (1 - dx) // 2]
        else:
            src, dst = y_out.at[up], y_in.at[up]
        return pltpu.make_async_remote_copy(
            src_ref=src,
            dst_ref=dst,
            send_sem=y_send.at[up, dx + 1],
            recv_sem=y_recv.at[up, 1 - dx],
            device_id=device(dx, 1 if up else -1),
            device_id_type=MESH,
        )

    def shift_of(s):
        return 1 if s < STEPS - 1 else 1 - STEPS

    def streamed(s, p, cx, row):
        pops = {}
        for cz in (-1, 0, 1):
            for cy in (-1, 0, 1):
                value = post[s, number(cx, cy, cz), p + 1 - cx, pl.ds(PAD + row + shift_of(s) - cz, 8), :]
                if cy:
                    value = pltpu.roll(value, cy % 128, axis=1)
                pops[number(cx, cy, cz)] = value
        return pops

    def place_far(s, j):
        row = pl.multiple_of(8 * j, 8)
        for p in (0, 1):
            for index, value in streamed(s, p, 1 - 2 * p, row).items():
                f[index, p, pl.ds(row, 8), :] = value

    def relax(s, to):
        ahead = 0 if s else 0
        behind = 1 if s == STEPS - 1 else 2

        def body(j, carry):
            row = pl.multiple_of(8 * j, 8)
            again = jnp.where(j == 0, PAD + depth, jnp.where(j == tiles - 1, 0, PAD + row))
            again = pl.multiple_of(again, 8)
            if s:

                @pl.when(j == tiles // 2 - 1)
                def _():
                    for up in (0, 1):
                        x_copy(s - 1, up, 1).wait_recv()

            far = [streamed(s - 1, p, 1 - 2 * p, row) if s and not ahead else {} for p in (0, 1)]
            before = [
                [far[p][i] if i in far[p] else f[i, p, pl.ds(row, 8), :] for i in range(27)]
                for p in (0, 1)
            ]
            if ahead:
                place_far(s - 1, jnp.minimum(j + 1, tiles - 1))
            place_own(s, to, jnp.maximum(j - behind, 2 - behind))
            for p in (0, 1):
                pops = before[p]
                fluid = mask[p, pl.ds(row + s, 8), :] == 1
                after = collide(pops)
                for index in range(27):
                    value = jnp.where(fluid, after[index], pops[26 - index])
                    post[s, index, p + 1, pl.ds(PAD + row, 8), :] = value
                    post[s, index, p + 1, pl.ds(again, 8), :] = value
            if s:

                @pl.when(j % (tiles // 2) == tiles // 2 - 1)
                def _():
                    for up in (0, 1):
                        x_copy(s, up, j // (tiles // 2)).start()

            return carry

        if s:
            for up in (0, 1):
                x_copy(s - 1, up, 0).wait_recv()
            wrap_faces(s - 1, PAD, PAD + depth)
            if ahead:
                place_far(s - 1, 0)
        lax.fori_loop(0, tiles, body, 0)

    def finish_own(s, to):
        def body(k, carry):
            j = lax.rem(tiles - 1 + k, tiles) if s == STEPS - 1 else tiles - 2 + k
            place_own(s, to, j)
            return carry

        lax.fori_loop(0, 2, body, 0)

    def wrap_faces(s, start, end):
        for there, lo in ((0, 18), (3, 0)):
            for index in range(lo, lo + NINE):
                post[s, index, there, end : end + 8, :] = post[s, index, there, start : start + 8, :]

    def make_rim():
        def gather(index, tile):
            for v in (0, 1):
                packed = None
                for low in (0, 1):
                    for p in (0, 1):
                        start = 64 * low + 16 * (p + 1)
                        value = turn(tile(2 * v + low, p), start - 122)
                        here = (lane >= start) & (lane < start + 16)
                        packed = value if packed is None else jnp.where(here, value, packed)
                rim[index, v] = packed

        def body(third, carry):
            for k in range(3):
                index = 3 * third + k
                gather(index, lambda j, p: f[index, p, 8 * j : 8 * j + 8, :])
            return carry

        lax.fori_loop(0, NINE, body, 0)
        gather(MASK, lambda j, p: mask[p, 8 * j : 8 * j + 8, :].astype(jnp.float32))
        for v in (0, 1):
            pops = [rim[index, v] for index in range(27)]
            after = collide(pops)
            fluid = rim[MASK, v] == 1.0
            for index in range(27):
                rim[index, v] = jnp.where(fluid, after[index], pops[26 - index])

    def own_part(index, cy, v):
        value = None
        for shift, lanes in OWN[cy]:
            moved = turn(rim[index, v], shift)
            value = moved if value is None else jnp.where(among(lanes, (1, 2)), moved, value)
        return value

    def make_messages():
        for up in (0, 1):
            packed = [[jnp.zeros((8, 128), jnp.float32)] * 2 for _ in range(3)]
            for what, (pair, quarter) in SLOTS.items():
                right, around = quarter % 2, quarter // 2
                for cy in (-1, 0, 1):
                    if what is None and cy:
                        continue
                    index = number(what[0], cy, what[1]) if what else MASK
                    shift, (low, high), _, _ = SENT[up][cy]
                    here = among((low + 8 * right, high + 8 * right), (3, 0) if around else (1, 2))
                    for v in (0, 1):
                        value = turn(rim[index, v], shift + 8 * right + 32 * around)
                        packed[pair][v] = jnp.where(here, value, packed[pair][v])
            for pair in range(3):
                for v in (0, 1):
                    y_out[up, pair, v] = packed[pair][v]

    def from_side(tile, what, cy, up, across, planes, value):
        quarter = SLOTS[what][1]
        _, _, shift, lanes = SENT[up][cy]
        moved = turn(tile, shift - 8 * (quarter % 2) - 32 * (quarter // 2) + across)
        return jnp.where(among(lanes, planes), moved, value)

    def send_fringe(s):
        for up in (0, 1):
            for pair in range(3):
                for v in (0, 1):
                    packed = None
                    for q in range(4 * pair, min(4 * pair + 4, NINE)):
                        value = turn(fringe[18 * up + q, v], 16 * (q % 4 - 1 - up))
                        packed = value if packed is None else jnp.where(plane == q % 4, value, packed)
                    e_out[s, up, pair, v] = packed
            e_copy(s, up).start()

    def receive_fringe(s):
        for up in (0, 1):
            e_copy(s, up).wait_recv()
            there = 0 if up else 3
            for q in range(NINE):
                index = 18 * up + q
                for v in (0, 1):
                    moved = turn(e_in[s, up, q // 4, v], 16 * (there - q % 4))
                    fringe[index, v] = jnp.where(plane == there, moved, fringe[index, v])

    def receive_sides():
        for up in (0, 1):
            for dx in (-1, 0, 1):
                y_copy(up, dx).wait_recv()
        for v in (0, 1):
            for what, (pair, _) in SLOTS.items():
                if what is None:
                    value = own_part(MASK, 0, v)
                    for up in (0, 1):
                        value = from_side(y_in[up, pair, v], what, 0, up, 0, (1, 2), value)
                    fringe_mask[v] = value
                    continue
                cx, cz = what
                for cy in (-1, 0, 1):
                    value = fringe[number(cx, cy, cz), v]
                    for up in (0, 1):
                        value = from_side(y_in[up, pair, v], what, cy, up, 0, (1, 2), value)
                        if cx:
                            near, there = (0, 0) if cx > 0 else (1, 3)
                            value = from_side(d_in[up, near, v], what, cy, up, -32 * cx, (there,), value)
                    fringe[number(cx, cy, cz), v] = value

    def moved_fringe(index):
        cx, cz = index // 9 - 1, index % 3 - 1
        pair = [turn(fringe[index, v], 16 * cx) for v in (0, 1)]
        if cz == 0:
            return pair
        pair = [pltpu.roll(value, cz % 8, axis=0) for value in pair]
        other = [turn(value, 64) for value in pair]
        first, second = (other[::-1], other) if cz > 0 else (other, other[::-1])
        edge = line == (0 if cz > 0 else 7)
        return [
            jnp.where(edge, jnp.where(lane < 64, first[v], second[v]), pair[v]) for v in (0, 1)
        ]

    def step_fringe():
        pops = [moved_fringe(index) for index in range(27)]
        for v in (0, 1):
            before = [pair[v] for pair in pops]
            after = collide(before)
            fluid = fringe_mask[v] == 1.0
            for index in range(27):
                value = jnp.where(fluid, after[index], before[26 - index])
                fringe[index, v] = turn(value, index // 3 % 3 - 1)

    def place_fringe(far):
        for index in range(27):
            cx = index // 9 - 1
            planes = [p for p in (0, 1) if (cx == 1 - 2 * p) == far]
            if not planes:
                continue
            pair = moved_fringe(index)
            for j in range(tiles):
                for p in planes:
                    start = 64 * (j % 2) + 16 * (p + 1)
                    left = turn(pair[j // 2], -start - 2)
                    right = turn(pair[j // 2], 125 - start - 10)
                    value = out[index, p, 8 * j : 8 * j + 8, :]
                    value = jnp.where(lane < 3, left, jnp.where(lane >= 125, right, value))
                    out[index, p, 8 * j : 8 * j + 8, :] = value

    def place_own(s, to, j):
        row = pl.multiple_of(8 * j, 8)
        for p in (0, 1):
            for cx in (0, 2 * p - 1):
                for cy in (-1, 0, 1):
                    for cz in (-1, 0, 1):
                        index = number(cx, cy, cz)
                        start = PAD + row + shift_of(s) - cz
                        value = post[s, index, p + 1 - cx, pl.ds(start, 8), :]
                        if cy:
                            value = pltpu.roll(value, cy % 128, axis=1)
                        to[index, p, pl.ds(row, 8), :] = value

    def place_faces(s, to):
        for up in (0, 1):
            x_copy(s, up, 0).wait_recv()
        for j in range(1, tiles + 1):
            if j == tiles // 2:
                for up in (0, 1):
                    x_copy(s, up, 1).wait_recv()
            if j == tiles:
                wrap_faces(s, depth, 0)
            row = 8 * (j % tiles)
            for p in (0, 1):
                for index, value in streamed(s, p, 1 - 2 * p, row).items():
                    to[index, p, row : row + 8, :] = value

    load_mask.wait()
    mask[:, depth : depth + 8, :] = mask[:, 0:8, :]
    for j in range(tiles):
        load(j).wait()
    make_rim()
    make_messages()

    def send_sides():
        for up in (0, 1):
            for dx in (0, -1, 1):
                y_copy(up, dx).start()

    @pl.when(odd == 1)
    def _():
        pl.semaphore_wait(barrier, len(ALONG_X) + len(ACROSS))
        tell(ready, ACROSS)
        send_sides()

    relax(0, f)

    @pl.when(odd == 0)
    def _():
        pl.semaphore_wait(barrier, len(ALONG_X))

    for index in range(27):
        for v in (0, 1):
            fringe[index, v] = own_part(index, index // 3 % 3 - 1, v)
    for j in (0, 1):
        for up in (0, 1):
            x_copy(0, up, j).start()
    send_fringe(0)
    finish_own(0, f)
    relax(1, f)
    finish_own(1, f)

    @pl.when(odd == 0)
    def _():
        pl.semaphore_wait(ready, len(ACROSS))
        send_sides()

    receive_fringe(0)
    receive_sides()
    step_fringe()
    send_fringe(1)
    relax(2, out)
    receive_fringe(1)
    step_fringe()
    send_fringe(2)
    finish_own(2, out)
    place_fringe(False)
    for up in (0, 1):
        for dx in (-1, 0, 1):
            y_copy(up, dx).wait_send()
        for s in range(STEPS):
            e_copy(s, up).wait_send()
            for j in (0, 1):
                x_copy(s, up, j).wait_send()
    place_faces(2, out)
    receive_fringe(2)
    place_fringe(True)


def solution(mesh):
    count_x, count_y = mesh.shape["gx"], mesh.shape["gy"]

    def on_device(populations, fluid_mask):
        width_x, depth, width_y = fluid_mask.shape
        tall = depth + 2 * PAD

        def body(*refs):
            kernel(count_x, count_y, *refs)

        return pl.pallas_call(
            body,
            out_shape=pltpu.VMEM(populations.shape, jnp.float32),
            in_specs=[pl.BlockSpec(memory_space=pltpu.HBM)] * 2,
            out_specs=pl.BlockSpec(memory_space=pltpu.VMEM),
            scratch_shapes=[
                pltpu.VMEM(populations.shape, jnp.float32),
                pltpu.VMEM((width_x, depth + 8, width_y), jnp.int32),
                pltpu.VMEM((STEPS, 27, width_x + 2, tall, width_y), jnp.float32),
                pltpu.VMEM((MASK + 1, 2, 8, 128), jnp.float32),
                pltpu.VMEM((27, 2, 8, 128), jnp.float32),
                pltpu.VMEM((2, 8, 128), jnp.float32),
                pltpu.VMEM((2, 3, 2, 8, 128), jnp.float32),
                pltpu.VMEM((2, 3, 2, 8, 128), jnp.float32),
                pltpu.VMEM((2, 2, 2, 8, 128), jnp.float32),
                pltpu.VMEM((STEPS, 2, 3, 2, 8, 128), jnp.float32),
                pltpu.VMEM((STEPS, 2, 3, 2, 8, 128), jnp.float32),
                pltpu.SemaphoreType.REGULAR,
                pltpu.SemaphoreType.DMA((depth // 8 + 1,)),
                pltpu.SemaphoreType.DMA((STEPS, 2, 2)),
                pltpu.SemaphoreType.DMA((STEPS, 2, 2)),
                pltpu.SemaphoreType.DMA((STEPS, 2)),
                pltpu.SemaphoreType.DMA((STEPS, 2)),
                pltpu.SemaphoreType.DMA((2, 3)),
                pltpu.SemaphoreType.DMA((2, 3)),
            ],
            compiler_params=pltpu.CompilerParams(
                collective_id=0, has_side_effects=True, vmem_limit_bytes=60 * 2**20
            ),
            cost_estimate=pl.CostEstimate(
                flops=500 * STEPS * fluid_mask.size,
                bytes_accessed=8 * populations.size,
                transcendentals=0,
            ),
            name="lattice_steps",
        )(populations, fluid_mask)

    in_specs = (P(None, "gx", None, "gy"), P("gx", None, "gy"))
    out_specs = P(None, "gx", None, "gy")
    return jax.shard_map(
        on_device, mesh=mesh, in_specs=in_specs, out_specs=out_specs, check_vma=False
    )
```

time: 34.1 us -> 31.9 us (0.935)
  Pallas kernels: 33 us -> 30.8 us
    pallas_call x1, Pallas kernels: 33 us -> 30.8 us  [on_device(): pl.pallas_call(body, out_shape=pltpu.VMEM(populations.shape, jnp.float32)...]
where the time goes in v4:
time: 31.9 us; the launch traced here: 31.8 us
  Pallas kernels  30.8 us (97%)
  local copies, waits for them, and re-layouts  0.91 us (3%)
    pallas_call x1, Pallas kernels, on_device(): pl.pallas_call(body, out_shape=pltpu.VMEM(populations.shape, jnp.float32)...  30.8 us
    unnamed x1, local copies, waits for them, and re-layouts  0.91 us

profile of v4, /device:TPU:1, one launch (start us, length us, event | category | flops | bytes accessed | tf_op | source)
XLA Modules:
  0.0 31.8 jit_solution(1405452094527403064)
XLA Ops:
  0.0 30.8 %lattice_steps.1 = f32[27,2,32,128]{3,2,1,0:T(8,128)S(1)} custom-call(f32[27,2,32,128]{3,2,1,0:T(8,128)} %refs_0_.1, s32[2,32,128]{2,1,0:T(8,128)} %refs_1_.1), custom_call_target="tpu_custom_call" | custom-call | flops 12288000 | bytes 1769472 | tf_op jit(solution)/shard_map/lattice_steps/pallas_call | solution.py:539
  30.9 0.9 %copy.4 = f32[27,2,32,128]{3,2,1,0:T(8,128)} copy(f32[27,2,32,128]{3,2,1,0:T(8,128)S(1)} %lattice_steps.1) | data formatting | bytes 1769472

commit v5 on v4

--- a/solution.py
+++ b/solution.py
@@ -488,12 +488,12 @@
     def _():
         pl.semaphore_wait(barrier, len(ALONG_X))
 
+    for j in (0, 1):
+        for up in (0, 1):
+            x_copy(0, up, j).start()
     for index in range(27):
         for v in (0, 1):
             fringe[index, v] = own_part(index, index // 3 % 3 - 1, v)
-    for j in (0, 1):
-        for up in (0, 1):
-            x_copy(0, up, j).start()
     send_fringe(0)
     finish_own(0, f)
     relax(1, f)

time: 31.9 us -> 31.2 us (0.978)
  Pallas kernels: 30.8 us -> 30.2 us
    pallas_call x1, Pallas kernels: 30.8 us -> 30.2 us  [on_device(): pl.pallas_call(body, out_shape=pltpu.VMEM(populations.shape, jnp.float32)...]
where the time goes in v5:
time: 31.2 us; the launch traced here: 31.1 us
  Pallas kernels  30.2 us (97%)
  local copies, waits for them, and re-layouts  0.91 us (3%)
    pallas_call x1, Pallas kernels, on_device(): pl.pallas_call(body, out_shape=pltpu.VMEM(populations.shape, jnp.float32)...  30.2 us
    unnamed x1, local copies, waits for them, and re-layouts  0.91 us

profile of v5, /device:TPU:1, one launch (start us, length us, event | category | flops | bytes accessed | tf_op | source)
XLA Modules:
  0.0 31.1 jit_solution(16256939430146393321)
XLA Ops:
  0.0 30.2 %lattice_steps.1 = f32[27,2,32,128]{3,2,1,0:T(8,128)S(1)} custom-call(f32[27,2,32,128]{3,2,1,0:T(8,128)} %refs_0_.1, s32[2,32,128]{2,1,0:T(8,128)} %refs_1_.1), custom_call_target="tpu_custom_call" | custom-call | flops 12288000 | bytes 1769472 | tf_op jit(solution)/shard_map/lattice_steps/pallas_call | solution.py:539
  30.2 0.9 %copy.4 = f32[27,2,32,128]{3,2,1,0:T(8,128)} copy(f32[27,2,32,128]{3,2,1,0:T(8,128)S(1)} %lattice_steps.1) | data formatting | bytes 1769472

commit v6 on v5

--- a/solution.py
+++ b/solution.py
@@ -355,25 +355,29 @@
         moved = turn(tile, shift - 8 * (quarter % 2) - 32 * (quarter // 2) + across)
         return jnp.where(among(lanes, planes), moved, value)
 
+    def part_of(tile):
+        if tile == 4:
+            return [(NINE - 1, v, v) for v in (0, 1)]
+        return [(4 * (tile // 2) + k, tile % 2, k) for k in range(4)]
+
     def send_fringe(s):
         for up in (0, 1):
-            for pair in range(3):
-                for v in (0, 1):
-                    packed = None
-                    for q in range(4 * pair, min(4 * pair + 4, NINE)):
-                        value = turn(fringe[18 * up + q, v], 16 * (q % 4 - 1 - up))
-                        packed = value if packed is None else jnp.where(plane == q % 4, value, packed)
-                    e_out[s, up, pair, v] = packed
+            for tile in range(5):
+                packed = None
+                for q, v, quarter in part_of(tile):
+                    value = turn(fringe[18 * up + q, v], 16 * (quarter - 1 - up))
+                    packed = value if packed is None else jnp.where(plane == quarter, value, packed)
+                e_out[s, up, tile] = packed
             e_copy(s, up).start()
 
     def receive_fringe(s):
         for up in (0, 1):
             e_copy(s, up).wait_recv()
             there = 0 if up else 3
-            for q in range(NINE):
-                index = 18 * up + q
-                for v in (0, 1):
-                    moved = turn(e_in[s, up, q // 4, v], 16 * (there - q % 4))
+            for tile in range(5):
+                for q, v, quarter in part_of(tile):
+                    index = 18 * up + q
+                    moved = turn(e_in[s, up, tile], 16 * (there - quarter))
                     fringe[index, v] = jnp.where(plane == there, moved, fringe[index, v])
 
     def receive_sides():
@@ -469,7 +473,8 @@
     for j in range(tiles):
         load(j).wait()
     make_rim()
-    make_messages()
+
+    pl.when(odd == 1)(make_messages)
 
     def send_sides():
         for up in (0, 1):
@@ -495,14 +500,15 @@
         for v in (0, 1):
             fringe[index, v] = own_part(index, index // 3 % 3 - 1, v)
     send_fringe(0)
+    pl.when(odd == 0)(make_messages)
     finish_own(0, f)
     relax(1, f)
-    finish_own(1, f)
-
     @pl.when(odd == 0)
     def _():
         pl.semaphore_wait(ready, len(ACROSS))
         send_sides()
+
+    finish_own(1, f)
 
     receive_fringe(0)
     receive_sides()
@@ -551,8 +557,8 @@
                 pltpu.VMEM((2, 3, 2, 8, 128), jnp.float32),
                 pltpu.VMEM((2, 3, 2, 8, 128), jnp.float32),
                 pltpu.VMEM((2, 2, 2, 8, 128), jnp.float32),
-                pltpu.VMEM((STEPS, 2, 3, 2, 8, 128), jnp.float32),
-                pltpu.VMEM((STEPS, 2, 3, 2, 8, 128), jnp.float32),
+                pltpu.VMEM((STEPS, 2, 5, 8, 128), jnp.float32),
+                pltpu.VMEM((STEPS, 2, 5, 8, 128), jnp.float32),
                 pltpu.SemaphoreType.REGULAR,
                 pltpu.SemaphoreType.DMA((depth // 8 + 1,)),
                 pltpu.SemaphoreType.DMA((STEPS, 2, 2)),

time: 31.2 us -> 31.1 us (level)
  no operation moved by 1% of the time
where the time goes in v6:
time: 31.1 us; the launch traced here: 30.9 us
  Pallas kernels  30 us (96%)
  local copies, waits for them, and re-layouts  0.91 us (3%)
    pallas_call x1, Pallas kernels, on_device(): pl.pallas_call(body, out_shape=pltpu.VMEM(populations.shape, jnp.float32)...  30 us
    unnamed x1, local copies, waits for them, and re-layouts  0.91 us

profile of v6, /device:TPU:1, one launch (start us, length us, event | category | flops | bytes accessed | tf_op | source)
XLA Modules:
  0.0 30.9 jit_solution(10833092871408933805)
XLA Ops:
  0.0 30.0 %lattice_steps.1 = f32[27,2,32,128]{3,2,1,0:T(8,128)S(1)} custom-call(f32[27,2,32,128]{3,2,1,0:T(8,128)} %refs_0_.1, s32[2,32,128]{2,1,0:T(8,128)} %refs_1_.1), custom_call_target="tpu_custom_call" | custom-call | flops 12288000 | bytes 1769472 | tf_op jit(solution)/shard_map/lattice_steps/pallas_call | solution.py:545
  30.0 0.9 %copy.4 = f32[27,2,32,128]{3,2,1,0:T(8,128)} copy(f32[27,2,32,128]{3,2,1,0:T(8,128)S(1)} %lattice_steps.1) | data formatting | bytes 1769472
